TPU v7x, 768 devices: a whole 4x8x12 slice. The times are simulated.
768 devices in a mesh: grp: 8 (over x, core), dp: 96 (over z, y).
Axes of the slice: x: 4, y: 8, z: 12, core: 2. Of those that a mesh axis runs over, the one named last changes fastest.
Arguments:
- queries: bfloat16 [98304, 256], P(('grp', 'dp')), may hold values from -11 to 11
- item_vecs: bfloat16 [122880, 256], P(('grp', 'dp')), may hold values from -1 to 1
- log_q: bfloat16 [122880], P(('grp', 'dp')), may hold values from -10 to -7
- weights: bfloat16 [98304], P(('grp', 'dp')), may hold values from 0.3 to 12
- item_owner: int32 [122880, 1], P(('grp', 'dp')), may hold values from 0 to 95; in each aligned block of 160 rows (0 to 159, 160 to 319, ...) at most 2 rows name the same one
- item_row: int32 [122880], P(('grp', 'dp')), may hold values from 0 to 1023
Outputs:
- query_grad: bfloat16 [98304, 256], P(('grp', 'dp'))
- table_grad: float32 [786432, 256], P(('grp', 'dp'))
Inputs may be any that keep to these rules, and one draw needn't show every extreme that they name: `item_owner`: among the items of one block of 160 rows no owner is named more than 2 times, and in some blocks an owner is named exactly 2 times.
All inputs are finite; a program needn't handle non-finite values.
Results may differ from a plain program's by a relative error of at most 0.012.
Values may be sent and summed in bfloat16 or wider, within the bound.
A program may use at most 32 MiB of HBM per device.

v0:
```python
import jax
import jax.numpy as jnp
from jax import lax
from jax.sharding import PartitionSpec as P

ROWS_DEV = 1024


def rows_by_rows(left, right):
    return lax.dot_general(
        left, right, (((1,), (1,)), ((), ())), preferred_element_type=jnp.float32
    )


def cols_by_rows(left, right):
    return lax.dot_general(
        left, right, (((0,), (0,)), ((), ())), preferred_element_type=jnp.float32
    )


def own_rows_grad(queries, weights, candidates, item_bias, norm, mine, per_item, groups):
    local_rows = queries.shape[0]
    logits = rows_by_rows(queries, candidates) - item_bias.astype(jnp.float32)[None, :]
    shares = jax.nn.softmax(logits, axis=1)
    target = mine * per_item + jnp.arange(local_rows, dtype=jnp.int32)
    columns = jnp.arange(groups * per_item, dtype=jnp.int32)
    positive = (columns[None, :] == target[:, None]).astype(jnp.float32)
    factor = weights.astype(jnp.float32) * norm
    return (factor[:, None] * (shares - positive)).astype(jnp.bfloat16)


def shards(queries, item_vecs, log_q, weights, item_owner, item_row):
    local_rows, width = queries.shape
    per_item = item_vecs.shape[0]
    groups = lax.axis_size("grp")
    owners = lax.axis_size("dp")
    mine = lax.axis_index("grp")
    total = lax.psum(jnp.sum(weights.astype(jnp.float32)), ("grp", "dp"))
    norm = local_rows * groups * owners / total
    candidates, item_bias = (
        lax.all_gather(item_vecs, "grp", axis=0, tiled=True),
        lax.all_gather(log_q, "grp", axis=0, tiled=True),
    )
    logit_grad = own_rows_grad(
        queries, weights, candidates, item_bias, norm, mine, per_item, groups
    )
    query_grad = jnp.dot(logit_grad, candidates, preferred_element_type=jnp.float32).astype(
        jnp.bfloat16
    )
    item_grad = lax.psum_scatter(
        cols_by_rows(logit_grad, queries), "grp", scatter_dimension=0, tiled=True
    ).astype(jnp.bfloat16)
    capacity = max(2, (per_item + owners - 1) // owners)
    owner = item_owner[:, 0]
    member = (owner[:, None] == jnp.arange(owners, dtype=jnp.int32)[None, :]).astype(jnp.int32)
    earlier = jnp.cumsum(member, axis=0) - member
    place = jnp.sum(earlier * member, axis=1)
    target_slot = owner * capacity + place
    send_rows = jnp.zeros((owners * capacity, width), jnp.bfloat16).at[target_slot].set(item_grad)
    send_ids = jnp.full((owners * capacity,), ROWS_DEV, jnp.int32).at[target_slot].set(item_row)
    got_rows, got_ids = (
        lax.all_to_all(
            send_rows.reshape(owners, capacity, width),
            "dp",
            split_axis=0,
            concat_axis=0,
            tiled=True,
        ),
        lax.all_to_all(
            send_ids.reshape(owners, capacity), "dp", split_axis=0, concat_axis=0, tiled=True
        ),
    )
    table_grad = (
        jnp.zeros((ROWS_DEV, width), jnp.float32)
        .at[got_ids.reshape(-1)]
        .add(got_rows.reshape(-1, width).astype(jnp.float32), mode="drop")
    )
    return (query_grad, table_grad)


def solution(mesh):
    in_specs = (
        P(("grp", "dp"), None),
        P(("grp", "dp"), None),
        P(("grp", "dp")),
        P(("grp", "dp")),
        P(("grp", "dp"), None),
        P(("grp", "dp")),
    )
    out_specs = (P(("grp", "dp"), None), P(("grp", "dp"), None))
    return jax.shard_map(shards, mesh=mesh, in_specs=in_specs, out_specs=out_specs, check_vma=False)
```

profile of v0, /device:TPU:1, one launch (start us, length us, event | category | flops | bytes accessed | tf_op | source)
XLA Modules:
  0.0 233.4 jit_solution(3661630069809064598)
XLA Ops:
  7.2 0.0 copy-start
  7.2 0.0 reduce-scatter.2.cloned.1.call-start
  7.2 1.3 convert_reduce_fusion
  8.5 120.4 %psum.7 = f32[]{:T(128)} all-reduce(f32[]{:T(128)} %convert_reduce_fusion), channel_id=1, replica_groups=mesh['grp'=8,'dp'=96] {'grp','dp'}, use_global_device_ids=true, to_apply=%region_1.0 | all-reduce | flops 1 | bytes 8 | tf_op jit(solution)/shard_map/psum | solution.py:38
  129.6 0.7 convert_multiply_fusion
  130.3 1.3 dynamic-slice
  132.2 0.9 dynamic-update-slice
  133.1 12.4 %all-reduce.1 = bf16[1280]{0:T(1024)(128)(2,1)S(1)} all-reduce(bf16[1280]{0:T(1024)(128)(2,1)S(1)} %dynamic-update-slice), channel_id=1, replica_groups=mesh['grp'=8,'dp'=96] {'grp'}, use_global_device_ids=true, to_apply=%add.1 | all-reduce | flops 1280 | bytes 5120
  145.5 14.2 %all_gather.6 = bf16[1280,256]{1,0:T(8,128)(2,1)S(1)} all-gather(bf16[160,256]{1,0:T(8,128)(2,1)} %param.7), channel_id=1, replica_groups=mesh['grp'=8,'dp'=96] {'grp'}, dimensions={0}, use_global_device_ids=true | all-gather | bytes 737280 | tf_op jit(solution)/shard_map/all_gather | solution.py:41
  159.7 0.0 copy-done
  159.7 0.5 fusion.10
  160.2 0.3 fusion
  160.4 0.4 multiply_convert_fusion
  160.8 0.0 copy-start.1
  160.8 1.4 fusion.11
  162.2 0.0 reduce-scatter.2.cloned.1.call-update
  162.3 0.0 copy-done.1
  162.3 0.6 reduce-window.6
  163.0 0.2 slice_reduce_fusion
  163.2 0.1 bitcast_bitcast_fusion
  163.3 1.2 scatter_custom_fusion
  164.6 0.8 all_to_all.9
  165.4 8.5 %all-to-all-start = ((s32[96,1,2]{2,1,0:T(1,128)}), s32[96,1,2]{2,1,0:T(1,128)S(1)}, u32[]{:S(2)}, u32[]{:S(2)}) async-start(s32[96,1,2]{2,1,0:T(1,128)} %bitcast.5), calls=%async_computation | async-start | bytes 98304 | tf_op jit(solution)/shard_map/all_to_all | solution.py:69
  173.9 19.6 %reduce-scatter.2.cloned.1.call-done = f32[160,256]{1,0:T(8,128)} async-done(((f32[1280,256]{1,0:T(8,128)}), f32[160,256]{1,0:T(8,128)}) %reduce-scatter.2.cloned.1.call-update) | async-done | bytes 163856 | tf_op jit(solution)/shard_map/reduce_scatter | solution.py:50
  193.5 1.5 scatter_custom_fusion.1
  195.0 0.7 reshape.69
  195.7 0.0 all-to-all-done
  195.7 14.6 %all-to-all-start.1 = ((bf16[96,2,256]{2,1,0:T(2,128)(2,1)}), bf16[96,2,256]{2,1,0:T(2,128)(2,1)S(1)}, u32[]{:S(2)}, u32[]{:S(2)}) async-start(bf16[96,2,256]{2,1,0:T(2,128)(2,1)} %reshape.69), calls=%async_computation.2 | async-start | bytes 196608 | tf_op jit(solution)/shard_map/all_to_all | solution.py:62
  210.4 0.9 convolution_convert_fusion
  211.2 0.6 broadcast.65
  211.8 0.8 reduce.5
  212.7 0.1 reshape.68
  212.8 11.1 %all-to-all-done.1 = bf16[96,2,256]{2,1,0:T(2,128)(2,1)S(1)} async-done(((bf16[96,2,256]{2,1,0:T(2,128)(2,1)}), bf16[96,2,256]{2,1,0:T(2,128)(2,1)S(1)}, u32[]{:S(2)}, u32[]{:S(2)}) %all-to-all-start.1) | async-done | bytes 98336 | tf_op jit(solution)/shard_map/all_to_all | solution.py:62
  224.0 2.6 %scatter_custom_fusion.2 = f32[1024,256]{1,0:T(8,128)} fusion(s32[192]{0:T(256)S(1)} %bitcast.31, f32[192,256]{1,0:T(8,128)S(1)} %reshape.92, f32[]{:T(128)} %constant.13.clone.1), kind=kCustom, calls=%fused_computation.9 | custom fusion | flops 49152 | bytes 1048580 | tf_op jit(solution)/shard_map/scatter-add | solution.py:76
  (11 shorter events, 0.2 us)
Async XLA Ops:
  7.2 152.6 %copy-start = (bf16[128,256]{1,0:T(8,128)(2,1)S(1)}, bf16[128,256]{1,0:T(8,128)(2,1)}, u32[]{:S(2)}) copy-start(bf16[128,256]{1,0:T(8,128)(2,1)} %param.6) | copy-start | bytes 196612
  7.2 186.3 %reduce-scatter.2.cloned.1.call-start = ((), (), s32[]{:S(2)}) async-start(), calls=%async_computation.3 | async-start | bytes 1474560 | tf_op jit(solution)/shard_map/reduce_scatter | solution.py:50
  160.8 1.5 copy-start.1
  165.4 30.4 %all-to-all-start = ((s32[96,1,2]{2,1,0:T(1,128)}), s32[96,1,2]{2,1,0:T(1,128)S(1)}, u32[]{:S(2)}, u32[]{:S(2)}) async-start(s32[96,1,2]{2,1,0:T(1,128)} %bitcast.5), calls=%async_computation | async-start | bytes 98304 | tf_op jit(solution)/shard_map/all_to_all | solution.py:69
  195.7 28.2 %all-to-all-start.1 = ((bf16[96,2,256]{2,1,0:T(2,128)(2,1)}), bf16[96,2,256]{2,1,0:T(2,128)(2,1)S(1)}, u32[]{:S(2)}, u32[]{:S(2)}) async-start(bf16[96,2,256]{2,1,0:T(2,128)(2,1)} %reshape.69), calls=%async_computation.2 | async-start | bytes 196608 | tf_op jit(solution)/shard_map/all_to_all | solution.py:62
Sparse Core Ops, SparseCore 0:
  162.4 31.0 reduce-scatter.1
where the time goes:
time: 236 us; the launch traced here: 233 us
  blocking collectives  147 us (62%)
  waiting for transfers between devices  30.7 us (13%)
  starting transfers between devices  23.2 us (10%)
  between operations  15.5 us (7%)
  other arithmetic  8.35 us (4%)
  local copies, waits for them, and re-layouts  5.77 us (2%)
  matrix products  2.77 us (1%)
    psum x1, blocking collectives, shards(): total = lax.psum(jnp.sum(weights.astype(jnp.float32)), ('grp', 'dp'))  120 us
    reduce_scatter x1, waiting for transfers between devices, shards(): lax.psum_scatter(cols_by_rows(logit_grad, queries), 'grp', scatter_dimens...  19.6 us
    all_to_all x1, starting transfers between devices, shards(): lax.all_to_all(send_rows.reshape(owners, capacity, width), 'dp', split_ax...  14.6 us
    all_gather x1, blocking collectives, shards(): lax.all_gather(item_vecs, 'grp', axis=0, tiled=True)  14.2 us
    unnamed x1, blocking collectives  12.4 us
    all_to_all x1, waiting for transfers between devices, shards(): lax.all_to_all(send_rows.reshape(owners, capacity, width), 'dp', split_ax...  11.1 us
    all_to_all x1, starting transfers between devices, shards(): lax.all_to_all(send_ids.reshape(owners, capacity), 'dp', split_axis=0, co...  8.54 us
  transfers between devices with their start and end apart: 3, of which 2 were waited for; matrix products, arithmetic and copies ran while one was open for 3% of the time, Pallas kernels for 0%

commit v1 on v0

v1 whole, which is shorter than its diff:
```python
import functools

import jax
import jax.numpy as jnp
from jax import lax
from jax.experimental import pallas as pl
from jax.experimental.pallas import tpu as pltpu
from jax.sharding import PartitionSpec as P

N_X = 4
N_GRP = 8
N_Z = 12
N_Y = 8
B_DEV = 128
PER_ITEM = 160
PAD_ITEM = 176
ROWS_DEV = 1024
D = 256
BATCH = 98304
MESH = pl.DeviceIdType.MESH
HIGHEST = lax.Precision.HIGHEST


def nt_dot(left, right, precision=None):
    return lax.dot_general(
        left, right, (((1,), (1,)), ((), ())), precision=precision, preferred_element_type=jnp.float32
    )


def tn_dot(left, right):
    return lax.dot_general(left, right, (((0,), (0,)), ((), ())), preferred_element_type=jnp.float32)


def iota(shape, dim):
    return lax.broadcasted_iota(jnp.int32, shape, dim)


def kernel(
    q_ref, it_ref, lq_ref, w_ref, own_ref, row_ref,
    dq_ref, tab_ref,
    items_all, q_all, logits, probs, cross, grads, stats,
    ids1_send, ids1_recv, ids1_flat, ids2_send, ids2_recv,
    slots, perm, member, send1, recv1, send2, recv2,
    it_send_sem, it_recv_sem, q_send_sem, q_recv_sem, st_send_sem, st_recv_sem,
    i1_send_sem, i1_recv_sem, i2_send_sem, i2_recv_sem,
    r1_send_sem, r1_recv_sem, r2_send_sem, r2_recv_sem,
):
    g = lax.axis_index("grp")
    d = lax.axis_index("dp")
    z, y = d // N_Y, d % N_Y
    x, c = g // 2, g % 2
    sib = 2 * x + 1 - c
    ahead = 1 - 2 * c

    barrier = pltpu.get_barrier_semaphore()

    def greet_grp(j, carry):
        pl.semaphore_signal(barrier, inc=1, device_id={"grp": (g + j) % N_GRP}, device_id_type=MESH)
        return carry

    def greet_z(j, carry):
        pl.semaphore_signal(barrier, inc=1, device_id={"dp": ((z + j) % N_Z) * N_Y + y}, device_id_type=MESH)
        return carry

    def greet_y(j, carry):
        pl.semaphore_signal(barrier, inc=1, device_id={"dp": z * N_Y + (y + j) % N_Y}, device_id_type=MESH)
        return carry

    lax.fori_loop(1, N_GRP, greet_grp, 0)
    lax.fori_loop(1, N_Z, greet_z, 0)
    lax.fori_loop(1, N_Y, greet_y, 0)

    log_q = lq_ref[...].astype(jnp.float32)
    weights = w_ref[...].astype(jnp.float32)
    owner_i = own_ref[...]
    row_i = row_ref[...]
    items_all[g, 0:PER_ITEM, :] = it_ref[...]
    padded_lq = jnp.concatenate([log_q, jnp.zeros((1, D - PER_ITEM), jnp.float32)], axis=1)
    items_all[g, PER_ITEM:PAD_ITEM, :] = jnp.broadcast_to(padded_lq, (16, D)).astype(jnp.bfloat16)
    q_all[g] = q_ref[...]

    owner = owner_i.astype(jnp.float32)
    sub, lane = iota((PER_ITEM, PER_ITEM), 0), iota((PER_ITEM, PER_ITEM), 1)
    eye = sub == lane
    owner_col = jnp.sum(jnp.where(eye, owner, 0.0), axis=1, keepdims=True)
    lq_col = jnp.sum(jnp.where(eye, log_q, 0.0), axis=1, keepdims=True)
    same = jnp.where((owner_col == owner) & (sub < lane), 1.0, 0.0)
    place = jnp.sum(same, axis=0, keepdims=True).astype(jnp.int32)
    dest_z = owner_i // N_Y
    slot = owner_i * 2 + place
    slot_z = slot - dest_z * (2 * N_Y)

    kind = iota((48, PER_ITEM), 0) // 16
    sub48 = iota((48, PER_ITEM), 0) % 16
    part = jnp.where(kind == 0, row_i // 32, jnp.where(kind == 1, row_i % 32, 1)).astype(jnp.float32)
    left = jnp.where(sub48 == dest_z, part, 0.0).astype(jnp.bfloat16)
    right = jnp.where(iota((128, PER_ITEM), 0) == slot_z, 1.0, 0.0).astype(jnp.bfloat16)
    found = nt_dot(left, right)
    ids1 = found[0:16] * 32.0 + found[16:32] + found[32:48]
    ids1 = jnp.where(iota((16, 128), 1) == 2 * N_Y, jnp.sum(weights, axis=1, keepdims=True), ids1)
    for k in range(N_Z):
        ids1_send[k] = ids1[k : k + 1]
    ids1_recv[z] = ids1_send[z]

    pl.semaphore_wait(barrier, (N_GRP - 1) + (N_Z - 1) + (N_Y - 1))

    def block_copy(buf, block, target, send_sem, recv_sem, index):
        return pltpu.make_async_remote_copy(
            src_ref=buf.at[block],
            dst_ref=buf.at[block],
            send_sem=send_sem.at[index],
            recv_sem=recv_sem.at[block],
            device_id={"grp": target},
            device_id_type=MESH,
        )

    def chip(dx):
        return (x + dx + N_X) % N_X

    behind_x, ahead_x, far_x = chip(-ahead), chip(ahead), chip(2)
    behind_g, ahead_g, far_g = 2 * behind_x + c, 2 * ahead_x + c, 2 * far_x + c
    sent = []

    def send(buf, block, target, sems, index):
        copy = block_copy(buf, block, target, sems[0], sems[1], index)
        copy.start()
        sent.append(copy)

    def arrived(buf, block, sems):
        block_copy(buf, block, sib, sems[0], sems[1], 0).wait_recv()

    it_sems = (it_send_sem, it_recv_sem)
    q_sems = (q_send_sem, q_recv_sem)

    def first_sends(buf, sems):
        send(buf, g, ahead_g, sems, 0)
        send(buf, g, behind_g, sems, 1)
        send(buf, g, sib, sems, 2)

    first_sends(items_all, it_sems)

    def ids1_copy(j):
        zt = (z + j) % N_Z
        return pltpu.make_async_remote_copy(
            src_ref=ids1_send.at[zt],
            dst_ref=ids1_recv.at[z],
            send_sem=i1_send_sem,
            recv_sem=i1_recv_sem,
            device_id={"dp": zt * N_Y + y},
            device_id_type=MESH,
        )

    def start_ids1(j, carry):
        ids1_copy(j).start()
        return carry

    lax.fori_loop(1, N_Z, start_ids1, 0)
    first_sends(q_all, q_sems)

    slots[...] = jnp.where(iota((2 * N_Z * N_Y, PER_ITEM), 0) == slot, 1.0, 0.0).astype(jnp.bfloat16)
    pr, pc = iota((N_Y * 32, 2 * N_Z * N_Y), 0), iota((N_Y * 32, 2 * N_Z * N_Y), 1)
    in_y = pr % 32
    perm[...] = jnp.where(
        (in_y < 2 * N_Z) & (pc == (in_y // 2) * (2 * N_Y) + (pr // 32) * 2 + in_y % 2), 1.0, 0.0
    ).astype(jnp.bfloat16)

    ones = jnp.ones((B_DEV, D), jnp.bfloat16)
    diag = iota((PER_ITEM, D), 0) == iota((PER_ITEM, D), 1)

    def block_logits(block, top):
        lq = items_all[block, PER_ITEM:PAD_ITEM, :].astype(jnp.float32)[0:1]
        bias = jnp.where(diag, lq, 0.0).astype(jnp.bfloat16)
        value = nt_dot(items_all[block, 0:PER_ITEM, :], q_ref[...]) - nt_dot(bias, ones)
        logits[block] = value
        here = jnp.max(value, axis=0, keepdims=True)
        return here if top is None else jnp.maximum(top, here)

    def block_cross(block):
        cross[block] = nt_dot(it_ref[...], q_all[block]) - lq_col

    top = block_logits(g, None)
    block_cross(g)

    arrived(items_all, behind_g, it_sems)
    send(items_all, behind_g, ahead_g, it_sems, 3)
    send(items_all, behind_g, sib, it_sems, 4)
    arrived(items_all, ahead_g, it_sems)
    send(items_all, ahead_g, sib, it_sems, 5)
    top = block_logits(behind_g, top)
    top = block_logits(ahead_g, top)

    pltpu.make_async_copy(ids1_recv.at[pl.ds(0, N_Z - 1)], ids1_recv.at[pl.ds(0, N_Z - 1)], i1_recv_sem).wait()
    ids1_flat[...] = jnp.zeros((16, 128), jnp.float32)
    for k in range(N_Z):
        ids1_flat[k : k + 1, :] = ids1_recv[k]
    got1 = ids1_flat[...]
    y_sub, l_lane = iota((N_Y, 128), 0), iota((N_Y, 128), 1)
    z_sub, s_lane = iota((16, D), 0), iota((16, D), 1)
    ids2 = jnp.zeros((N_Y, D), jnp.float32)
    for k in range(2):
        pick = jnp.where(l_lane == 2 * y_sub + k, 1.0, 0.0)
        spread = jnp.where(s_lane == y * 32 + 2 * z_sub + k, 1.0, 0.0)
        picked = nt_dot(pick, got1, HIGHEST)
        ids2 = ids2 + jnp.dot(picked, spread, precision=HIGHEST, preferred_element_type=jnp.float32)
    summed = jnp.sum(got1, axis=0, keepdims=True)
    w_z = jnp.sum(jnp.where(iota((1, 128), 1) == 2 * N_Y, summed, 0.0), axis=1, keepdims=True)
    ids2 = jnp.where(iota((N_Y, D), 1) == y * 32 + 24, w_z, ids2)
    for k in range(N_Y):
        ids2_send[k] = ids2[k : k + 1]
    ids2_recv[y] = ids2_send[y]

    def ids2_copy(j):
        yt = (y + j) % N_Y
        return pltpu.make_async_remote_copy(
            src_ref=ids2_send.at[yt],
            dst_ref=ids2_recv.at[y],
            send_sem=i2_send_sem,
            recv_sem=i2_recv_sem,
            device_id={"dp": z * N_Y + yt},
            device_id_type=MESH,
        )

    def start_ids2(j, carry):
        ids2_copy(j).start()
        return carry

    lax.fori_loop(1, N_Y, start_ids2, 0)

    arrived(q_all, behind_g, q_sems)
    send(q_all, behind_g, ahead_g, q_sems, 3)
    send(q_all, behind_g, sib, q_sems, 4)
    arrived(q_all, ahead_g, q_sems)
    send(q_all, ahead_g, sib, q_sems, 5)
    arrived(items_all, far_g, it_sems)
    send(items_all, far_g, sib, it_sems, 6)
    top = block_logits(far_g, top)
    block_cross(behind_g)
    block_cross(ahead_g)
    for other in (x, behind_x, ahead_x, far_x):
        block = 2 * other + 1 - c
        arrived(items_all, block, it_sems)
        top = block_logits(block, top)
    arrived(q_all, far_g, q_sems)
    send(q_all, far_g, sib, q_sems, 6)

    total = jnp.zeros((1, B_DEV), jnp.float32)
    for b in range(N_GRP):
        shifted = jnp.exp(logits[b] - top)
        logits[b] = shifted
        total = total + jnp.sum(shifted, axis=0, keepdims=True)

    pltpu.make_async_copy(ids2_recv.at[pl.ds(0, N_Y - 1)], ids2_recv.at[pl.ds(0, N_Y - 1)], i2_recv_sem).wait()
    got2 = ids2_recv[0]
    for k in range(1, N_Y):
        got2 = got2 + ids2_recv[k]
    in_block = iota((1, D), 1) % 32
    slab = jnp.sum(jnp.where(in_block == 24, got2, 0.0), axis=1, keepdims=True)
    row_ids = jnp.where(in_block < 2 * N_Z, got2, 0.0).astype(jnp.int32)

    stats[g, :, 0:128] = top
    stats[g, :, 128:256] = 1.0 / total
    stats[g, :, 256:384] = weights
    stats[g, :, 384:512] = jnp.broadcast_to(slab, (1, 128))

    def stats_copy(j):
        return block_copy(stats, g, (g + j) % N_GRP, st_send_sem, st_recv_sem, j)

    def start_stats(j, carry):
        stats_copy(j).start()
        return carry

    lax.fori_loop(1, N_GRP, start_stats, 0)

    block_cross(far_g)
    for other in (x, behind_x, ahead_x, far_x):
        block = 2 * other + 1 - c
        arrived(q_all, block, q_sems)
        block_cross(block)

    def wait_stats(j, carry):
        block_copy(stats, (g + j) % N_GRP, sib, st_send_sem, st_recv_sem, 0).wait_recv()
        return carry

    lax.fori_loop(1, N_GRP, wait_stats, 0)

    weight_sum = stats[0, :, 384:512]
    for b in range(1, N_GRP):
        weight_sum = weight_sum + stats[b, :, 384:512]
    norm = BATCH / weight_sum
    pos_sub, pos_lane = iota((PER_ITEM, B_DEV), 0), iota((PER_ITEM, B_DEV), 1)
    for b in range(N_GRP):
        share = jnp.exp(cross[b] - stats[b, :, 0:128]) * stats[b, :, 128:256]
        share = share - jnp.where(pos_sub + b * PER_ITEM == pos_lane + g * PER_ITEM, 1.0, 0.0)
        grads[:, b * B_DEV : (b + 1) * B_DEV] = (stats[b, :, 256:384] * norm * share).astype(jnp.bfloat16)
    item_grad = jnp.dot(
        grads[...], q_all[...].reshape(N_GRP * B_DEV, D), preferred_element_type=jnp.float32
    ).astype(jnp.bfloat16)
    placed = jnp.dot(slots[...], item_grad, preferred_element_type=jnp.float32)
    send1[...] = placed.astype(jnp.bfloat16).reshape(N_Z, 2 * N_Y, D)

    def rows1_copy(j):
        zt = (z + j) % N_Z
        return pltpu.make_async_remote_copy(
            src_ref=send1.at[zt],
            dst_ref=recv1.at[z],
            send_sem=r1_send_sem,
            recv_sem=r1_recv_sem,
            device_id={"dp": zt * N_Y + y},
            device_id_type=MESH,
        )

    def start_rows1(j, carry):
        rows1_copy(j).start()
        return carry

    lax.fori_loop(1, N_Z, start_rows1, 0)
    recv1[z] = send1[z]

    member[...] = jnp.where(iota((ROWS_DEV, D), 0) + 1 == row_ids, 1.0, 0.0).astype(jnp.bfloat16)
    factor = weights * norm
    inverse = 1.0 / total
    for b in range(N_GRP):
        share = logits[b] * inverse
        share = share - jnp.where(pos_sub + b * PER_ITEM == pos_lane + g * PER_ITEM, 1.0, 0.0)
        probs[b, 0:PER_ITEM, :] = (factor * share).astype(jnp.bfloat16)
        probs[b, PER_ITEM:PAD_ITEM, :] = jnp.zeros((PAD_ITEM - PER_ITEM, B_DEV), jnp.bfloat16)
    dq_ref[...] = tn_dot(
        probs[...].reshape(N_GRP * PAD_ITEM, B_DEV), items_all[...].reshape(N_GRP * PAD_ITEM, D)
    ).astype(jnp.bfloat16)

    pltpu.make_async_copy(recv1.at[pl.ds(0, N_Z - 1)], recv1.at[pl.ds(0, N_Z - 1)], r1_recv_sem).wait()
    turned = jnp.dot(perm[...], recv1[...].reshape(2 * N_Z * N_Y, D), preferred_element_type=jnp.float32)
    send2[...] = turned.astype(jnp.bfloat16).reshape(N_Y, 32, D)

    def rows2_copy(j):
        yt = (y + j) % N_Y
        return pltpu.make_async_remote_copy(
            src_ref=send2.at[yt],
            dst_ref=recv2.at[y],
            send_sem=r2_send_sem,
            recv_sem=r2_recv_sem,
            device_id={"dp": z * N_Y + yt},
            device_id_type=MESH,
        )

    def start_rows2(j, carry):
        rows2_copy(j).start()
        return carry

    lax.fori_loop(1, N_Y, start_rows2, 0)
    recv2[y] = send2[y]

    for copy in sent:
        copy.wait_send()
    def wait_stats_sent(j, carry):
        stats_copy(j).wait_send()
        return carry

    lax.fori_loop(1, N_GRP, wait_stats_sent, 0)
    pltpu.make_async_copy(ids1_send.at[pl.ds(0, N_Z - 1)], ids1_send.at[pl.ds(0, N_Z - 1)], i1_send_sem).wait()
    pltpu.make_async_copy(ids2_send.at[pl.ds(0, N_Y - 1)], ids2_send.at[pl.ds(0, N_Y - 1)], i2_send_sem).wait()
    pltpu.make_async_copy(send1.at[pl.ds(0, N_Z - 1)], send1.at[pl.ds(0, N_Z - 1)], r1_send_sem).wait()
    pltpu.make_async_copy(recv2.at[pl.ds(0, N_Y - 1)], recv2.at[pl.ds(0, N_Y - 1)], r2_recv_sem).wait()
    tab_ref[...] = jnp.dot(member[...], recv2[...].reshape(N_Y * 32, D), preferred_element_type=jnp.float32)
    pltpu.make_async_copy(send2.at[pl.ds(0, N_Y - 1)], send2.at[pl.ds(0, N_Y - 1)], r2_send_sem).wait()


def shards(queries, item_vecs, log_q, weights, item_owner, item_row):
    vmem = pl.BlockSpec(memory_space=pltpu.VMEM)
    bf16, f32 = jnp.bfloat16, jnp.float32
    dma = pltpu.SemaphoreType.DMA
    return pl.pallas_call(
        kernel,
        out_shape=(
            jax.ShapeDtypeStruct((B_DEV, D), bf16),
            jax.ShapeDtypeStruct((ROWS_DEV, D), f32),
        ),
        in_specs=[vmem] * 6,
        out_specs=(vmem, vmem),
        scratch_shapes=[
            pltpu.VMEM((N_GRP, PAD_ITEM, D), bf16),
            pltpu.VMEM((N_GRP, B_DEV, D), bf16),
            pltpu.VMEM((N_GRP, PER_ITEM, B_DEV), f32),
            pltpu.VMEM((N_GRP, PAD_ITEM, B_DEV), bf16),
            pltpu.VMEM((N_GRP, PER_ITEM, B_DEV), f32),
            pltpu.VMEM((PER_ITEM, N_GRP * B_DEV), bf16),
            pltpu.VMEM((N_GRP, 1, 512), f32),
            pltpu.VMEM((N_Z, 1, 128), f32),
            pltpu.VMEM((N_Z, 1, 128), f32),
            pltpu.VMEM((16, 128), f32),
            pltpu.VMEM((N_Y, 1, D), f32),
            pltpu.VMEM((N_Y, 1, D), f32),
            pltpu.VMEM((2 * N_Z * N_Y, PER_ITEM), bf16),
            pltpu.VMEM((N_Y * 32, 2 * N_Z * N_Y), bf16),
            pltpu.VMEM((ROWS_DEV, D), bf16),
            pltpu.VMEM((N_Z, 2 * N_Y, D), bf16),
            pltpu.VMEM((N_Z, 2 * N_Y, D), bf16),
            pltpu.VMEM((N_Y, 32, D), bf16),
            pltpu.VMEM((N_Y, 32, D), bf16),
            dma((7,)), dma((N_GRP,)),
            dma((7,)), dma((N_GRP,)),
            dma((N_GRP,)), dma((N_GRP,)),
            dma, dma, dma, dma, dma, dma, dma, dma,
        ],
        compiler_params=pltpu.CompilerParams(
            collective_id=0, has_side_effects=True, vmem_limit_bytes=32 * 1024 * 1024
        ),
    )(
        queries,
        item_vecs,
        log_q.reshape(1, PER_ITEM),
        weights.reshape(1, B_DEV),
        item_owner.reshape(1, PER_ITEM),
        item_row.reshape(1, PER_ITEM),
    )


def solution(mesh):
    in_specs = (
        P(("grp", "dp"), None),
        P(("grp", "dp"), None),
        P(("grp", "dp")),
        P(("grp", "dp")),
        P(("grp", "dp"), None),
        P(("grp", "dp")),
    )
    out_specs = (P(("grp", "dp"), None), P(("grp", "dp"), None))
    return jax.shard_map(shards, mesh=mesh, in_specs=in_specs, out_specs=out_specs, check_vma=False)
```

time: 236 us -> 52.2 us (0.22)
  blocking collectives: 147 us -> 0 us
  Pallas kernels: 0 us -> 46.6 us
  waiting for transfers between devices: 30.7 us -> 0 us
  starting transfers between devices: 23.2 us -> 0 us
  between operations: 15.5 us -> 0.66 us
  other arithmetic: 8.35 us -> 0 us
  matrix products: 2.77 us -> 0 us
    psum x1 -> x0, blocking collectives: 120 us -> none  [shards(): total = lax.psum(jnp.sum(weights.astype(jnp.float32)), ('grp', 'dp'))]
    pallas_call x0 -> x1, Pallas kernels: none -> 46.6 us  [shards(): pl.pallas_call(kernel, out_shape=(jax.ShapeDtypeStruct((B_DEV, D), bf16),...]
    all_to_all x2 -> x0, starting transfers between devices: 23.2 us -> none  [the longest x1 14.6 us: shards(): lax.all_to_all(send_rows.reshape(owners, capacity, width), 'dp', split_ax...]
    reduce_scatter x1 -> x0, waiting for transfers between devices: 19.6 us -> none  [shards(): lax.psum_scatter(cols_by_rows(logit_grad, queries), 'grp', scatter_dimens...]
    all_gather x1 -> x0, blocking collectives: 14.2 us -> none  [shards(): lax.all_gather(item_vecs, 'grp', axis=0, tiled=True)]
    unnamed x1 -> x0, blocking collectives: 12.4 us -> none
    all_to_all x2 -> x0, waiting for transfers between devices: 11.1 us -> none  [the longest x1 11.1 us: shards(): lax.all_to_all(send_rows.reshape(owners, capacity, width), 'dp', split_ax...]
    dot_general x3 -> x0, matrix products: 2.77 us -> none  [the longest x1 1.42 us: cols_by_rows(): lax.dot_general(left, right, (((0,), (0,)), ((), ())), preferred_element_...]
  transfers between devices with their start and end apart: 3 -> 0, of which waited for: 2 -> 0; matrix products, arithmetic and copies ran while one was open for 3% -> 0% of each run, Pallas kernels for 0% -> 0%
where the time goes in v1:
time: 52.2 us; the launch traced here: 51.9 us
  Pallas kernels  46.6 us (89%)
  local copies, waits for them, and re-layouts  4.65 us (9%)
  between operations  0.66 us (1%)
    pallas_call x1, Pallas kernels, shards(): pl.pallas_call(kernel, out_shape=(jax.ShapeDtypeStruct((B_DEV, D), bf16),...  46.6 us
    unnamed x14, local copies, waits for them, and re-layouts  4.64 us

profile of v1, /device:TPU:1, one launch (start us, length us, event | category | flops | bytes accessed | tf_op | source)
XLA Modules:
  0.0 51.9 jit_solution(17303754049038109162)
XLA Ops:
  0.6 0.0 copy-start.5
  0.6 0.0 copy-start.3
  0.7 0.6 %copy-done.5 = bf16[160]{0:T(256)(128)(2,1)S(1)} copy-done((bf16[160]{0:T(256)(128)(2,1)S(1)}, bf16[160]{0:T(256)(128)(2,1)}, u32[]{:S(2)}) %copy-start.5) | copy-done | bytes 344
  1.3 0.0 copy-start.2
  1.3 0.0 copy-start.4
  1.3 0.0 copy-done.3
  1.3 0.6 %copy-done.2 = s32[160,1]{0,1:T(1,128)S(1)} copy-done((s32[160,1]{0,1:T(1,128)S(1)}, s32[160,1]{0,1:T(1,128)}, u32[]{:S(2)}) %copy-start.2) | copy-done | bytes 664
  2.0 0.0 copy-done.4
  2.0 0.0 copy-start
  2.0 0.9 %copy-done = bf16[160,256]{1,0:T(8,128)(2,1)S(1)} copy-done((bf16[160,256]{1,0:T(8,128)(2,1)S(1)}, bf16[160,256]{1,0:T(8,128)(2,1)}, u32[]{:S(2)}) %copy-start) | copy-done | bytes 81944
  2.9 0.0 copy-start.1
  2.9 0.8 %copy-done.1 = bf16[128,256]{1,0:T(8,128)(2,1)S(1)} copy-done((bf16[128,256]{1,0:T(8,128)(2,1)S(1)}, bf16[128,256]{1,0:T(8,128)(2,1)}, u32[]{:S(2)}) %copy-start.1) | copy-done | bytes 65560
  3.7 46.6 %shard_map.77 = (bf16[128,256]{1,0:T(8,128)(2,1)S(1)}, f32[1024,256]{1,0:T(8,128)S(1)}) custom-call(bf16[128,256]{1,0:T(8,128)(2,1)S(1)} %copy-done.1, bf16[160,256]{1,0:T(8,128)(2,1)S(1)} %copy-done, bf16[1,160]{1,0:T(2,128)(2,1)S(1)} %reshape.16.lq_ref, bf16[1,128]{1,0:T(2,128)(2,1)S(1)} %bitcast.5, s32[1,160]{1,0:T(1,128)S(1)} %bitcast.3, ...), custom_call_target="tpu_custom_call" | custom-call | tf_op jit(solution)/shard_map/pallas_call | solution.py:372
  50.3 0.6 %copy.10 = bf16[128,256]{1,0:T(8,128)(2,1)} copy(bf16[128,256]{1,0:T(8,128)(2,1)S(1)} %get-tuple-element.4) | data formatting | bytes 131072
  51.0 1.0 %copy.11 = f32[1024,256]{1,0:T(8,128)} copy(f32[1024,256]{1,0:T(8,128)S(1)} %get-tuple-element.5) | data formatting | bytes 2097152
  (1 shorter events, 0.0 us)
Async XLA Ops:
  0.6 0.7 %copy-start.5 = (bf16[160]{0:T(256)(128)(2,1)S(1)}, bf16[160]{0:T(256)(128)(2,1)}, u32[]{:S(2)}) copy-start(bf16[160]{0:T(256)(128)(2,1)} %param.8) | copy-start | bytes 964
  0.6 0.7 %copy-start.3 = (s32[160]{0:T(256)S(1)}, s32[160]{0:T(256)}, u32[]{:S(2)}) copy-start(s32[160]{0:T(256)} %param.11) | copy-start | bytes 1924
  1.3 0.7 %copy-start.2 = (s32[160,1]{0,1:T(1,128)S(1)}, s32[160,1]{0,1:T(1,128)}, u32[]{:S(2)}) copy-start(s32[160,1]{0,1:T(1,128)} %param.10) | copy-start | bytes 1924
  1.3 0.7 %copy-start.4 = (bf16[128]{0:T(256)(128)(2,1)S(1)}, bf16[128]{0:T(256)(128)(2,1)}, u32[]{:S(2)}) copy-start(bf16[128]{0:T(256)(128)(2,1)} %param.9) | copy-start | bytes 772
  2.0 0.9 %copy-start = (bf16[160,256]{1,0:T(8,128)(2,1)S(1)}, bf16[160,256]{1,0:T(8,128)(2,1)}, u32[]{:S(2)}) copy-start(bf16[160,256]{1,0:T(8,128)(2,1)} %it_ref.1) | copy-start | bytes 245764
  2.9 0.8 %copy-start.1 = (bf16[128,256]{1,0:T(8,128)(2,1)S(1)}, bf16[128,256]{1,0:T(8,128)(2,1)}, u32[]{:S(2)}) copy-start(bf16[128,256]{1,0:T(8,128)(2,1)} %q_ref.1) | copy-start | bytes 196612

commit v2 on v1

--- a/solution.py
+++ b/solution.py
@@ -36,11 +36,13 @@
 
 
 def kernel(
-    q_ref, it_ref, lq_ref, w_ref, own_ref, row_ref,
+    q_hbm, it_hbm, lq_hbm, w_hbm, own_hbm, row_hbm,
     dq_ref, tab_ref,
+    lq_ref, w_ref, own_ref, row_ref, slabs,
     items_all, q_all, logits, probs, cross, grads, stats,
     ids1_send, ids1_recv, ids1_flat, ids2_send, ids2_recv,
     slots, perm, member, send1, recv1, send2, recv2,
+    in_sem, sl_send_sem, sl_recv_sem,
     it_send_sem, it_recv_sem, q_send_sem, q_recv_sem, st_send_sem, st_recv_sem,
     i1_send_sem, i1_recv_sem, i2_send_sem, i2_recv_sem,
     r1_send_sem, r1_recv_sem, r2_send_sem, r2_recv_sem,
@@ -52,6 +54,20 @@
     sib = 2 * x + 1 - c
     ahead = 1 - 2 * c
 
+    loads = [
+        pltpu.make_async_copy(src, dst, in_sem.at[i])
+        for i, (src, dst) in enumerate((
+            (it_hbm, items_all.at[g, pl.ds(0, PER_ITEM)]),
+            (q_hbm, q_all.at[g]),
+            (lq_hbm, lq_ref),
+            (w_hbm, w_ref),
+            (own_hbm, own_ref),
+            (row_hbm, row_ref),
+        ))
+    ]
+    for load in loads:
+        load.start()
+
     barrier = pltpu.get_barrier_semaphore()
 
     def greet_grp(j, carry):
@@ -70,14 +86,53 @@
     lax.fori_loop(1, N_Z, greet_z, 0)
     lax.fori_loop(1, N_Y, greet_y, 0)
 
-    log_q = lq_ref[...].astype(jnp.float32)
-    weights = w_ref[...].astype(jnp.float32)
+    for load in loads:
+        load.wait()
+    log_q = lq_ref[...].astype(jnp.float32).reshape(1, PER_ITEM)
+    padded_lq = jnp.concatenate([log_q, jnp.zeros((1, D - PER_ITEM), jnp.float32)], axis=1)
+    items_all[g, PER_ITEM:PAD_ITEM, :] = jnp.broadcast_to(padded_lq, (16, D)).astype(jnp.bfloat16)
+
+    pl.semaphore_wait(barrier, (N_GRP - 1) + (N_Z - 1) + (N_Y - 1))
+
+    def block_copy(buf, block, target, send_sem, recv_sem, index):
+        return pltpu.make_async_remote_copy(
+            src_ref=buf.at[block],
+            dst_ref=buf.at[block],
+            send_sem=send_sem.at[index],
+            recv_sem=recv_sem.at[block],
+            device_id={"grp": target},
+            device_id_type=MESH,
+        )
+
+    def chip(dx):
+        return (x + dx + N_X) % N_X
+
+    behind_x, ahead_x, far_x = chip(-ahead), chip(ahead), chip(2)
+    behind_g, ahead_g, far_g = 2 * behind_x + c, 2 * ahead_x + c, 2 * far_x + c
+    sent = []
+
+    def send(buf, block, target, sems, index):
+        copy = block_copy(buf, block, target, sems[0], sems[1], index)
+        copy.start()
+        sent.append(copy)
+
+    def arrived(buf, block, sems):
+        block_copy(buf, block, sib, sems[0], sems[1], 0).wait_recv()
+
+    it_sems = (it_send_sem, it_recv_sem)
+    q_sems = (q_send_sem, q_recv_sem)
+
+    def first_sends(buf, sems):
+        send(buf, g, ahead_g, sems, 0)
+        send(buf, g, behind_g, sems, 1)
+        send(buf, g, sib, sems, 2)
+
+    first_sends(items_all, it_sems)
+    first_sends(q_all, q_sems)
+
+    weights = w_ref[...].astype(jnp.float32).reshape(1, B_DEV)
     owner_i = own_ref[...]
     row_i = row_ref[...]
-    items_all[g, 0:PER_ITEM, :] = it_ref[...]
-    padded_lq = jnp.concatenate([log_q, jnp.zeros((1, D - PER_ITEM), jnp.float32)], axis=1)
-    items_all[g, PER_ITEM:PAD_ITEM, :] = jnp.broadcast_to(padded_lq, (16, D)).astype(jnp.bfloat16)
-    q_all[g] = q_ref[...]
 
     owner = owner_i.astype(jnp.float32)
     sub, lane = iota((PER_ITEM, PER_ITEM), 0), iota((PER_ITEM, PER_ITEM), 1)
@@ -102,42 +157,6 @@
         ids1_send[k] = ids1[k : k + 1]
     ids1_recv[z] = ids1_send[z]
 
-    pl.semaphore_wait(barrier, (N_GRP - 1) + (N_Z - 1) + (N_Y - 1))
-
-    def block_copy(buf, block, target, send_sem, recv_sem, index):
-        return pltpu.make_async_remote_copy(
-            src_ref=buf.at[block],
-            dst_ref=buf.at[block],
-            send_sem=send_sem.at[index],
-            recv_sem=recv_sem.at[block],
-            device_id={"grp": target},
-            device_id_type=MESH,
-        )
-
-    def chip(dx):
-        return (x + dx + N_X) % N_X
-
-    behind_x, ahead_x, far_x = chip(-ahead), chip(ahead), chip(2)
-    behind_g, ahead_g, far_g = 2 * behind_x + c, 2 * ahead_x + c, 2 * far_x + c
-    sent = []
-
-    def send(buf, block, target, sems, index):
-        copy = block_copy(buf, block, target, sems[0], sems[1], index)
-        copy.start()
-        sent.append(copy)
-
-    def arrived(buf, block, sems):
-        block_copy(buf, block, sib, sems[0], sems[1], 0).wait_recv()
-
-    it_sems = (it_send_sem, it_recv_sem)
-    q_sems = (q_send_sem, q_recv_sem)
-
-    def first_sends(buf, sems):
-        send(buf, g, ahead_g, sems, 0)
-        send(buf, g, behind_g, sems, 1)
-        send(buf, g, sib, sems, 2)
-
-    first_sends(items_all, it_sems)
 
     def ids1_copy(j):
         zt = (z + j) % N_Z
@@ -155,7 +174,6 @@
         return carry
 
     lax.fori_loop(1, N_Z, start_ids1, 0)
-    first_sends(q_all, q_sems)
 
     slots[...] = jnp.where(iota((2 * N_Z * N_Y, PER_ITEM), 0) == slot, 1.0, 0.0).astype(jnp.bfloat16)
     pr, pc = iota((N_Y * 32, 2 * N_Z * N_Y), 0), iota((N_Y * 32, 2 * N_Z * N_Y), 1)
@@ -170,13 +188,13 @@
     def block_logits(block, top):
         lq = items_all[block, PER_ITEM:PAD_ITEM, :].astype(jnp.float32)[0:1]
         bias = jnp.where(diag, lq, 0.0).astype(jnp.bfloat16)
-        value = nt_dot(items_all[block, 0:PER_ITEM, :], q_ref[...]) - nt_dot(bias, ones)
+        value = nt_dot(items_all[block, 0:PER_ITEM, :], q_all[g]) - nt_dot(bias, ones)
         logits[block] = value
         here = jnp.max(value, axis=0, keepdims=True)
         return here if top is None else jnp.maximum(top, here)
 
     def block_cross(block):
-        cross[block] = nt_dot(it_ref[...], q_all[block]) - lq_col
+        cross[block] = nt_dot(items_all[g, 0:PER_ITEM, :], q_all[block]) - lq_col
 
     top = block_logits(g, None)
     block_cross(g)
@@ -186,8 +204,41 @@
     send(items_all, behind_g, sib, it_sems, 4)
     arrived(items_all, ahead_g, it_sems)
     send(items_all, ahead_g, sib, it_sems, 5)
+    arrived(q_all, behind_g, q_sems)
+    send(q_all, behind_g, ahead_g, q_sems, 3)
+    send(q_all, behind_g, sib, q_sems, 4)
+    arrived(q_all, ahead_g, q_sems)
+    send(q_all, ahead_g, sib, q_sems, 5)
     top = block_logits(behind_g, top)
     top = block_logits(ahead_g, top)
+    arrived(items_all, far_g, it_sems)
+    send(items_all, far_g, sib, it_sems, 6)
+    top = block_logits(far_g, top)
+    arrived(q_all, far_g, q_sems)
+    send(q_all, far_g, sib, q_sems, 6)
+    for other in (x, behind_x, ahead_x, far_x):
+        block = 2 * other + 1 - c
+        arrived(items_all, block, it_sems)
+        top = block_logits(block, top)
+
+    total = jnp.zeros((1, B_DEV), jnp.float32)
+    for b in range(N_GRP):
+        shifted = jnp.exp(logits[b] - top)
+        logits[b] = shifted
+        total = total + jnp.sum(shifted, axis=0, keepdims=True)
+
+    stats[g, :, 0:128] = top
+    stats[g, :, 128:256] = 1.0 / total
+    stats[g, :, 256:384] = weights
+
+    def stats_copy(j):
+        return block_copy(stats, g, (g + j) % N_GRP, st_send_sem, st_recv_sem, j)
+
+    def start_stats(j, carry):
+        stats_copy(j).start()
+        return carry
+
+    lax.fori_loop(1, N_GRP, start_stats, 0)
 
     pltpu.make_async_copy(ids1_recv.at[pl.ds(0, N_Z - 1)], ids1_recv.at[pl.ds(0, N_Z - 1)], i1_recv_sem).wait()
     ids1_flat[...] = jnp.zeros((16, 128), jnp.float32)
@@ -226,51 +277,8 @@
 
     lax.fori_loop(1, N_Y, start_ids2, 0)
 
-    arrived(q_all, behind_g, q_sems)
-    send(q_all, behind_g, ahead_g, q_sems, 3)
-    send(q_all, behind_g, sib, q_sems, 4)
-    arrived(q_all, ahead_g, q_sems)
-    send(q_all, ahead_g, sib, q_sems, 5)
-    arrived(items_all, far_g, it_sems)
-    send(items_all, far_g, sib, it_sems, 6)
-    top = block_logits(far_g, top)
     block_cross(behind_g)
     block_cross(ahead_g)
-    for other in (x, behind_x, ahead_x, far_x):
-        block = 2 * other + 1 - c
-        arrived(items_all, block, it_sems)
-        top = block_logits(block, top)
-    arrived(q_all, far_g, q_sems)
-    send(q_all, far_g, sib, q_sems, 6)
-
-    total = jnp.zeros((1, B_DEV), jnp.float32)
-    for b in range(N_GRP):
-        shifted = jnp.exp(logits[b] - top)
-        logits[b] = shifted
-        total = total + jnp.sum(shifted, axis=0, keepdims=True)
-
-    pltpu.make_async_copy(ids2_recv.at[pl.ds(0, N_Y - 1)], ids2_recv.at[pl.ds(0, N_Y - 1)], i2_recv_sem).wait()
-    got2 = ids2_recv[0]
-    for k in range(1, N_Y):
-        got2 = got2 + ids2_recv[k]
-    in_block = iota((1, D), 1) % 32
-    slab = jnp.sum(jnp.where(in_block == 24, got2, 0.0), axis=1, keepdims=True)
-    row_ids = jnp.where(in_block < 2 * N_Z, got2, 0.0).astype(jnp.int32)
-
-    stats[g, :, 0:128] = top
-    stats[g, :, 128:256] = 1.0 / total
-    stats[g, :, 256:384] = weights
-    stats[g, :, 384:512] = jnp.broadcast_to(slab, (1, 128))
-
-    def stats_copy(j):
-        return block_copy(stats, g, (g + j) % N_GRP, st_send_sem, st_recv_sem, j)
-
-    def start_stats(j, carry):
-        stats_copy(j).start()
-        return carry
-
-    lax.fori_loop(1, N_GRP, start_stats, 0)
-
     block_cross(far_g)
     for other in (x, behind_x, ahead_x, far_x):
         block = 2 * other + 1 - c
@@ -283,15 +291,11 @@
 
     lax.fori_loop(1, N_GRP, wait_stats, 0)
 
-    weight_sum = stats[0, :, 384:512]
-    for b in range(1, N_GRP):
-        weight_sum = weight_sum + stats[b, :, 384:512]
-    norm = BATCH / weight_sum
     pos_sub, pos_lane = iota((PER_ITEM, B_DEV), 0), iota((PER_ITEM, B_DEV), 1)
     for b in range(N_GRP):
         share = jnp.exp(cross[b] - stats[b, :, 0:128]) * stats[b, :, 128:256]
         share = share - jnp.where(pos_sub + b * PER_ITEM == pos_lane + g * PER_ITEM, 1.0, 0.0)
-        grads[:, b * B_DEV : (b + 1) * B_DEV] = (stats[b, :, 256:384] * norm * share).astype(jnp.bfloat16)
+        grads[:, b * B_DEV : (b + 1) * B_DEV] = (stats[b, :, 256:384] * share).astype(jnp.bfloat16)
     item_grad = jnp.dot(
         grads[...], q_all[...].reshape(N_GRP * B_DEV, D), preferred_element_type=jnp.float32
     ).astype(jnp.bfloat16)
@@ -316,17 +320,46 @@
     lax.fori_loop(1, N_Z, start_rows1, 0)
     recv1[z] = send1[z]
 
+    pltpu.make_async_copy(ids2_recv.at[pl.ds(0, N_Y - 1)], ids2_recv.at[pl.ds(0, N_Y - 1)], i2_recv_sem).wait()
+    got2 = ids2_recv[0]
+    for k in range(1, N_Y):
+        got2 = got2 + ids2_recv[k]
+    in_block = iota((1, D), 1) % 32
+    slab = jnp.sum(jnp.where(in_block == 24, got2, 0.0), axis=1, keepdims=True)
+    row_ids = jnp.where(in_block < 2 * N_Z, got2, 0.0).astype(jnp.int32)
+
+    slabs[g] = jnp.broadcast_to(slab, (1, 128))
+
+    def slab_copy(j):
+        return block_copy(slabs, g, (g + j) % N_GRP, sl_send_sem, sl_recv_sem, j)
+
+    def start_slabs(j, carry):
+        slab_copy(j).start()
+        return carry
+
+    lax.fori_loop(1, N_GRP, start_slabs, 0)
+
     member[...] = jnp.where(iota((ROWS_DEV, D), 0) + 1 == row_ids, 1.0, 0.0).astype(jnp.bfloat16)
-    factor = weights * norm
     inverse = 1.0 / total
     for b in range(N_GRP):
         share = logits[b] * inverse
         share = share - jnp.where(pos_sub + b * PER_ITEM == pos_lane + g * PER_ITEM, 1.0, 0.0)
-        probs[b, 0:PER_ITEM, :] = (factor * share).astype(jnp.bfloat16)
+        probs[b, 0:PER_ITEM, :] = (weights * share).astype(jnp.bfloat16)
         probs[b, PER_ITEM:PAD_ITEM, :] = jnp.zeros((PAD_ITEM - PER_ITEM, B_DEV), jnp.bfloat16)
-    dq_ref[...] = tn_dot(
+    query_grad = tn_dot(
         probs[...].reshape(N_GRP * PAD_ITEM, B_DEV), items_all[...].reshape(N_GRP * PAD_ITEM, D)
-    ).astype(jnp.bfloat16)
+    )
+
+    def wait_slabs(j, carry):
+        block_copy(slabs, (g + j) % N_GRP, sib, sl_send_sem, sl_recv_sem, 0).wait_recv()
+        return carry
+
+    lax.fori_loop(1, N_GRP, wait_slabs, 0)
+    weight_sum = slabs[0]
+    for b in range(1, N_GRP):
+        weight_sum = weight_sum + slabs[b]
+    norm = BATCH / weight_sum[:, 0:1]
+    dq_ref[...] = (query_grad * norm).astype(jnp.bfloat16)
 
     pltpu.make_async_copy(recv1.at[pl.ds(0, N_Z - 1)], recv1.at[pl.ds(0, N_Z - 1)], r1_recv_sem).wait()
     turned = jnp.dot(perm[...], recv1[...].reshape(2 * N_Z * N_Y, D), preferred_element_type=jnp.float32)
@@ -354,6 +387,7 @@
         copy.wait_send()
     def wait_stats_sent(j, carry):
         stats_copy(j).wait_send()
+        slab_copy(j).wait_send()
         return carry
 
     lax.fori_loop(1, N_GRP, wait_stats_sent, 0)
@@ -361,7 +395,9 @@
     pltpu.make_async_copy(ids2_send.at[pl.ds(0, N_Y - 1)], ids2_send.at[pl.ds(0, N_Y - 1)], i2_send_sem).wait()
     pltpu.make_async_copy(send1.at[pl.ds(0, N_Z - 1)], send1.at[pl.ds(0, N_Z - 1)], r1_send_sem).wait()
     pltpu.make_async_copy(recv2.at[pl.ds(0, N_Y - 1)], recv2.at[pl.ds(0, N_Y - 1)], r2_recv_sem).wait()
-    tab_ref[...] = jnp.dot(member[...], recv2[...].reshape(N_Y * 32, D), preferred_element_type=jnp.float32)
+    tab_ref[...] = norm * jnp.dot(
+        member[...], recv2[...].reshape(N_Y * 32, D), preferred_element_type=jnp.float32
+    )
     pltpu.make_async_copy(send2.at[pl.ds(0, N_Y - 1)], send2.at[pl.ds(0, N_Y - 1)], r2_send_sem).wait()
 
 
@@ -375,16 +411,21 @@
             jax.ShapeDtypeStruct((B_DEV, D), bf16),
             jax.ShapeDtypeStruct((ROWS_DEV, D), f32),
         ),
-        in_specs=[vmem] * 6,
+        in_specs=[pl.BlockSpec(memory_space=pltpu.HBM)] * 6,
         out_specs=(vmem, vmem),
         scratch_shapes=[
+            pltpu.VMEM((PER_ITEM,), bf16),
+            pltpu.VMEM((B_DEV,), bf16),
+            pltpu.VMEM((1, PER_ITEM), jnp.int32),
+            pltpu.VMEM((1, PER_ITEM), jnp.int32),
+            pltpu.VMEM((N_GRP, 1, 128), f32),
             pltpu.VMEM((N_GRP, PAD_ITEM, D), bf16),
             pltpu.VMEM((N_GRP, B_DEV, D), bf16),
             pltpu.VMEM((N_GRP, PER_ITEM, B_DEV), f32),
             pltpu.VMEM((N_GRP, PAD_ITEM, B_DEV), bf16),
             pltpu.VMEM((N_GRP, PER_ITEM, B_DEV), f32),
             pltpu.VMEM((PER_ITEM, N_GRP * B_DEV), bf16),
-            pltpu.VMEM((N_GRP, 1, 512), f32),
+            pltpu.VMEM((N_GRP, 1, 384), f32),
             pltpu.VMEM((N_Z, 1, 128), f32),
             pltpu.VMEM((N_Z, 1, 128), f32),
             pltpu.VMEM((16, 128), f32),
@@ -397,6 +438,7 @@
             pltpu.VMEM((N_Z, 2 * N_Y, D), bf16),
             pltpu.VMEM((N_Y, 32, D), bf16),
             pltpu.VMEM((N_Y, 32, D), bf16),
+            dma((6,)), dma((N_GRP,)), dma((N_GRP,)),
             dma((7,)), dma((N_GRP,)),
             dma((7,)), dma((N_GRP,)),
             dma((N_GRP,)), dma((N_GRP,)),
@@ -405,14 +447,17 @@
         compiler_params=pltpu.CompilerParams(
             collective_id=0, has_side_effects=True, vmem_limit_bytes=32 * 1024 * 1024
         ),
-    )(
-        queries,
-        item_vecs,
-        log_q.reshape(1, PER_ITEM),
-        weights.reshape(1, B_DEV),
-        item_owner.reshape(1, PER_ITEM),
-        item_row.reshape(1, PER_ITEM),
-    )
+    )(*(
+        pltpu.with_memory_space_constraint(operand, pltpu.HBM)
+        for operand in (
+            queries,
+            item_vecs,
+            log_q,
+            weights,
+            item_owner.reshape(1, PER_ITEM),
+            item_row.reshape(1, PER_ITEM),
+        )
+    ))
 
 
 def solution(mesh):

time: 52.2 us -> 48.9 us (0.937)
  local copies, waits for them, and re-layouts: 4.65 us -> 1.6 us
  Pallas kernels: 46.6 us -> 45.9 us
    unnamed x14 -> x2, local copies, waits for them, and re-layouts: 4.64 us -> 1.6 us
    pallas_call x1, Pallas kernels: 46.6 us -> 45.9 us  [shards(): pl.pallas_call(kernel, out_shape=(jax.ShapeDtypeStruct((B_DEV, D), bf16),...]
where the time goes in v2:
time: 48.9 us; the launch traced here: 48.2 us
  Pallas kernels  45.9 us (94%)
  local copies, waits for them, and re-layouts  1.6 us (3%)
  between operations  0.64 us (1%)
    pallas_call x1, Pallas kernels, shards(): pl.pallas_call(kernel, out_shape=(jax.ShapeDtypeStruct((B_DEV, D), bf16),...  45.9 us
    unnamed x2, local copies, waits for them, and re-layouts  1.6 us

profile of v2, /device:TPU:1, one launch (start us, length us, event | category | flops | bytes accessed | tf_op | source)
XLA Modules:
  0.0 48.2 jit_solution(14335341965477370758)
XLA Ops:
  0.6 45.9 %shard_map.77 = (bf16[128,256]{1,0:T(8,128)(2,1)S(1)}, f32[1024,256]{1,0:T(8,128)S(1)}) custom-call(bf16[128,256]{1,0:T(8,128)(2,1)} %q_hbm.1, bf16[160,256]{1,0:T(8,128)(2,1)} %it_hbm.1, bf16[160]{0:T(256)(128)(2,1)} %lq_hbm.1, bf16[128]{0:T(256)(128)(2,1)} %w_hbm.1, s32[1,160]{1,0:T(1,128)} %bitcast.2, s32[1,160]{1,0:T(1,128)} %bitcast.3), custom_call_target="tpu_custom_call" | custom-call | tf_op jit(solution)/shard_map/pallas_call | solution.py:408
  46.6 0.6 %copy.10 = bf16[128,256]{1,0:T(8,128)(2,1)} copy(bf16[128,256]{1,0:T(8,128)(2,1)S(1)} %get-tuple-element.4) | data formatting | bytes 131072
  47.2 1.0 %copy.11 = f32[1024,256]{1,0:T(8,128)} copy(f32[1024,256]{1,0:T(8,128)S(1)} %get-tuple-element.5) | data formatting | bytes 2097152

commit v3 on v2

--- a/solution.py
+++ b/solution.py
@@ -38,11 +38,11 @@
 def kernel(
     q_hbm, it_hbm, lq_hbm, w_hbm, own_hbm, row_hbm,
     dq_ref, tab_ref,
-    lq_ref, w_ref, own_ref, row_ref, slabs,
+    lq_ref, w_ref, own_ref, row_ref,
     items_all, q_all, logits, probs, cross, grads, stats,
     ids1_send, ids1_recv, ids1_flat, ids2_send, ids2_recv,
     slots, perm, member, send1, recv1, send2, recv2,
-    in_sem, sl_send_sem, sl_recv_sem,
+    in_sem, z_sems, y_sems,
     it_send_sem, it_recv_sem, q_send_sem, q_recv_sem, st_send_sem, st_recv_sem,
     i1_send_sem, i1_recv_sem, i2_send_sem, i2_recv_sem,
     r1_send_sem, r1_recv_sem, r2_send_sem, r2_recv_sem,
@@ -74,25 +74,30 @@
         pl.semaphore_signal(barrier, inc=1, device_id={"grp": (g + j) % N_GRP}, device_id_type=MESH)
         return carry
 
-    def greet_z(j, carry):
-        pl.semaphore_signal(barrier, inc=1, device_id={"dp": ((z + j) % N_Z) * N_Y + y}, device_id_type=MESH)
-        return carry
-
-    def greet_y(j, carry):
-        pl.semaphore_signal(barrier, inc=1, device_id={"dp": z * N_Y + (y + j) % N_Y}, device_id_type=MESH)
-        return carry
-
     lax.fori_loop(1, N_GRP, greet_grp, 0)
-    lax.fori_loop(1, N_Z, greet_z, 0)
-    lax.fori_loop(1, N_Y, greet_y, 0)
+
+    def z_peer(step):
+        return {"dp": ((z + step + N_Z) % N_Z) * N_Y + y}
+
+    def y_peer(step):
+        return {"dp": z * N_Y + (y + step + N_Y) % N_Y}
+
+    def signal_pair(sem, peer, step):
+        pl.semaphore_signal(sem, inc=1, device_id=peer(step), device_id_type=MESH)
+        pl.semaphore_signal(sem, inc=1, device_id=peer(-step), device_id_type=MESH)
+
+    signal_pair(barrier, z_peer, 1)
+    signal_pair(barrier, y_peer, 1)
 
     for load in loads:
         load.wait()
     log_q = lq_ref[...].astype(jnp.float32).reshape(1, PER_ITEM)
+    weights = w_ref[...].astype(jnp.float32).reshape(1, B_DEV)
     padded_lq = jnp.concatenate([log_q, jnp.zeros((1, D - PER_ITEM), jnp.float32)], axis=1)
-    items_all[g, PER_ITEM:PAD_ITEM, :] = jnp.broadcast_to(padded_lq, (16, D)).astype(jnp.bfloat16)
-
-    pl.semaphore_wait(barrier, (N_GRP - 1) + (N_Z - 1) + (N_Y - 1))
+    padded_w = jnp.concatenate([weights, jnp.zeros((1, D - B_DEV), jnp.float32)], axis=1)
+    items_all[g, PER_ITEM:PAD_ITEM, :] = jnp.where(iota((16, D), 0) == 0, padded_lq, padded_w).astype(jnp.bfloat16)
+
+    pl.semaphore_wait(barrier, (N_GRP - 1) + 2 + 2)
 
     def block_copy(buf, block, target, send_sem, recv_sem, index):
         return pltpu.make_async_remote_copy(
@@ -129,8 +134,9 @@
 
     first_sends(items_all, it_sems)
     first_sends(q_all, q_sems)
-
-    weights = w_ref[...].astype(jnp.float32).reshape(1, B_DEV)
+    signal_pair(z_sems.at[0], z_peer, 1)
+    signal_pair(y_sems.at[0], y_peer, 1)
+
     owner_i = own_ref[...]
     row_i = row_ref[...]
 
@@ -152,29 +158,6 @@
     right = jnp.where(iota((128, PER_ITEM), 0) == slot_z, 1.0, 0.0).astype(jnp.bfloat16)
     found = nt_dot(left, right)
     ids1 = found[0:16] * 32.0 + found[16:32] + found[32:48]
-    ids1 = jnp.where(iota((16, 128), 1) == 2 * N_Y, jnp.sum(weights, axis=1, keepdims=True), ids1)
-    for k in range(N_Z):
-        ids1_send[k] = ids1[k : k + 1]
-    ids1_recv[z] = ids1_send[z]
-
-
-    def ids1_copy(j):
-        zt = (z + j) % N_Z
-        return pltpu.make_async_remote_copy(
-            src_ref=ids1_send.at[zt],
-            dst_ref=ids1_recv.at[z],
-            send_sem=i1_send_sem,
-            recv_sem=i1_recv_sem,
-            device_id={"dp": zt * N_Y + y},
-            device_id_type=MESH,
-        )
-
-    def start_ids1(j, carry):
-        ids1_copy(j).start()
-        return carry
-
-    lax.fori_loop(1, N_Z, start_ids1, 0)
-
     slots[...] = jnp.where(iota((2 * N_Z * N_Y, PER_ITEM), 0) == slot, 1.0, 0.0).astype(jnp.bfloat16)
     pr, pc = iota((N_Y * 32, 2 * N_Z * N_Y), 0), iota((N_Y * 32, 2 * N_Z * N_Y), 1)
     in_y = pr % 32
@@ -204,6 +187,10 @@
     send(items_all, behind_g, sib, it_sems, 4)
     arrived(items_all, ahead_g, it_sems)
     send(items_all, ahead_g, sib, it_sems, 5)
+    pl.semaphore_wait(z_sems.at[0], 2)
+    signal_pair(z_sems.at[1], z_peer, 2)
+    pl.semaphore_wait(y_sems.at[0], 2)
+    signal_pair(y_sems.at[1], y_peer, 2)
     arrived(q_all, behind_g, q_sems)
     send(q_all, behind_g, ahead_g, q_sems, 3)
     send(q_all, behind_g, sib, q_sems, 4)
@@ -214,6 +201,8 @@
     arrived(items_all, far_g, it_sems)
     send(items_all, far_g, sib, it_sems, 6)
     top = block_logits(far_g, top)
+    pl.semaphore_wait(z_sems.at[1], 2)
+    signal_pair(z_sems.at[2], z_peer, 2)
     arrived(q_all, far_g, q_sems)
     send(q_all, far_g, sib, q_sems, 6)
     for other in (x, behind_x, ahead_x, far_x):
@@ -229,7 +218,6 @@
 
     stats[g, :, 0:128] = top
     stats[g, :, 128:256] = 1.0 / total
-    stats[g, :, 256:384] = weights
 
     def stats_copy(j):
         return block_copy(stats, g, (g + j) % N_GRP, st_send_sem, st_recv_sem, j)
@@ -239,6 +227,91 @@
         return carry
 
     lax.fori_loop(1, N_GRP, start_stats, 0)
+
+    def block_weights(block):
+        return items_all[block, PER_ITEM:PAD_ITEM, 0:B_DEV].astype(jnp.float32)[1:2]
+
+    group_sum = jnp.zeros((1, 1), jnp.float32)
+    for b in range(N_GRP):
+        group_sum = group_sum + jnp.sum(block_weights(b), axis=1, keepdims=True)
+    ids1 = jnp.where(iota((16, 128), 1) == 2 * N_Y, group_sum, ids1)
+    for k in range(N_Z):
+        ids1_send[k] = ids1[k : k + 1]
+    ids1_recv[z] = ids1_send[z]
+
+
+    pl.semaphore_wait(z_sems.at[2], 2)
+    pl.semaphore_wait(y_sems.at[1], 2)
+
+    def ids1_copy(j):
+        zt = (z + j) % N_Z
+        return pltpu.make_async_remote_copy(
+            src_ref=ids1_send.at[zt],
+            dst_ref=ids1_recv.at[z],
+            send_sem=i1_send_sem,
+            recv_sem=i1_recv_sem,
+            device_id={"dp": zt * N_Y + y},
+            device_id_type=MESH,
+        )
+
+    def start_ids1(j, carry):
+        ids1_copy(j).start()
+        return carry
+
+    lax.fori_loop(1, N_Z, start_ids1, 0)
+
+    block_cross(behind_g)
+    block_cross(ahead_g)
+    block_cross(far_g)
+    for other in (x, behind_x, ahead_x, far_x):
+        block = 2 * other + 1 - c
+        arrived(q_all, block, q_sems)
+        block_cross(block)
+
+    def wait_stats(j, carry):
+        block_copy(stats, (g + j) % N_GRP, sib, st_send_sem, st_recv_sem, 0).wait_recv()
+        return carry
+
+    lax.fori_loop(1, N_GRP, wait_stats, 0)
+
+    pos_sub, pos_lane = iota((PER_ITEM, B_DEV), 0), iota((PER_ITEM, B_DEV), 1)
+    for b in range(N_GRP):
+        share = jnp.exp(cross[b] - stats[b, :, 0:128]) * stats[b, :, 128:256]
+        share = share - jnp.where(pos_sub + b * PER_ITEM == pos_lane + g * PER_ITEM, 1.0, 0.0)
+        grads[:, b * B_DEV : (b + 1) * B_DEV] = (block_weights(b) * share).astype(jnp.bfloat16)
+    item_grad = jnp.dot(
+        grads[...], q_all[...].reshape(N_GRP * B_DEV, D), preferred_element_type=jnp.float32
+    ).astype(jnp.bfloat16)
+    placed = jnp.dot(slots[...], item_grad, preferred_element_type=jnp.float32)
+    send1[...] = placed.astype(jnp.bfloat16).reshape(N_Z, 2 * N_Y, D)
+
+    def rows1_copy(j):
+        zt = (z + j) % N_Z
+        return pltpu.make_async_remote_copy(
+            src_ref=send1.at[zt],
+            dst_ref=recv1.at[z],
+            send_sem=r1_send_sem,
+            recv_sem=r1_recv_sem,
+            device_id={"dp": zt * N_Y + y},
+            device_id_type=MESH,
+        )
+
+    def start_rows1(j, carry):
+        rows1_copy(j).start()
+        return carry
+
+    lax.fori_loop(1, N_Z, start_rows1, 0)
+    recv1[z] = send1[z]
+
+    inverse = 1.0 / total
+    for b in range(N_GRP):
+        share = logits[b] * inverse
+        share = share - jnp.where(pos_sub + b * PER_ITEM == pos_lane + g * PER_ITEM, 1.0, 0.0)
+        probs[b, 0:PER_ITEM, :] = (weights * share).astype(jnp.bfloat16)
+        probs[b, PER_ITEM:PAD_ITEM, :] = jnp.zeros((PAD_ITEM - PER_ITEM, B_DEV), jnp.bfloat16)
+    query_grad = tn_dot(
+        probs[...].reshape(N_GRP * PAD_ITEM, B_DEV), items_all[...].reshape(N_GRP * PAD_ITEM, D)
+    )
 
     pltpu.make_async_copy(ids1_recv.at[pl.ds(0, N_Z - 1)], ids1_recv.at[pl.ds(0, N_Z - 1)], i1_recv_sem).wait()
     ids1_flat[...] = jnp.zeros((16, 128), jnp.float32)
@@ -277,90 +350,6 @@
 
     lax.fori_loop(1, N_Y, start_ids2, 0)
 
-    block_cross(behind_g)
-    block_cross(ahead_g)
-    block_cross(far_g)
-    for other in (x, behind_x, ahead_x, far_x):
-        block = 2 * other + 1 - c
-        arrived(q_all, block, q_sems)
-        block_cross(block)
-
-    def wait_stats(j, carry):
-        block_copy(stats, (g + j) % N_GRP, sib, st_send_sem, st_recv_sem, 0).wait_recv()
-        return carry
-
-    lax.fori_loop(1, N_GRP, wait_stats, 0)
-
-    pos_sub, pos_lane = iota((PER_ITEM, B_DEV), 0), iota((PER_ITEM, B_DEV), 1)
-    for b in range(N_GRP):
-        share = jnp.exp(cross[b] - stats[b, :, 0:128]) * stats[b, :, 128:256]
-        share = share - jnp.where(pos_sub + b * PER_ITEM == pos_lane + g * PER_ITEM, 1.0, 0.0)
-        grads[:, b * B_DEV : (b + 1) * B_DEV] = (stats[b, :, 256:384] * share).astype(jnp.bfloat16)
-    item_grad = jnp.dot(
-        grads[...], q_all[...].reshape(N_GRP * B_DEV, D), preferred_element_type=jnp.float32
-    ).astype(jnp.bfloat16)
-    placed = jnp.dot(slots[...], item_grad, preferred_element_type=jnp.float32)
-    send1[...] = placed.astype(jnp.bfloat16).reshape(N_Z, 2 * N_Y, D)
-
-    def rows1_copy(j):
-        zt = (z + j) % N_Z
-        return pltpu.make_async_remote_copy(
-            src_ref=send1.at[zt],
-            dst_ref=recv1.at[z],
-            send_sem=r1_send_sem,
-            recv_sem=r1_recv_sem,
-            device_id={"dp": zt * N_Y + y},
-            device_id_type=MESH,
-        )
-
-    def start_rows1(j, carry):
-        rows1_copy(j).start()
-        return carry
-
-    lax.fori_loop(1, N_Z, start_rows1, 0)
-    recv1[z] = send1[z]
-
-    pltpu.make_async_copy(ids2_recv.at[pl.ds(0, N_Y - 1)], ids2_recv.at[pl.ds(0, N_Y - 1)], i2_recv_sem).wait()
-    got2 = ids2_recv[0]
-    for k in range(1, N_Y):
-        got2 = got2 + ids2_recv[k]
-    in_block = iota((1, D), 1) % 32
-    slab = jnp.sum(jnp.where(in_block == 24, got2, 0.0), axis=1, keepdims=True)
-    row_ids = jnp.where(in_block < 2 * N_Z, got2, 0.0).astype(jnp.int32)
-
-    slabs[g] = jnp.broadcast_to(slab, (1, 128))
-
-    def slab_copy(j):
-        return block_copy(slabs, g, (g + j) % N_GRP, sl_send_sem, sl_recv_sem, j)
-
-    def start_slabs(j, carry):
-        slab_copy(j).start()
-        return carry
-
-    lax.fori_loop(1, N_GRP, start_slabs, 0)
-
-    member[...] = jnp.where(iota((ROWS_DEV, D), 0) + 1 == row_ids, 1.0, 0.0).astype(jnp.bfloat16)
-    inverse = 1.0 / total
-    for b in range(N_GRP):
-        share = logits[b] * inverse
-        share = share - jnp.where(pos_sub + b * PER_ITEM == pos_lane + g * PER_ITEM, 1.0, 0.0)
-        probs[b, 0:PER_ITEM, :] = (weights * share).astype(jnp.bfloat16)
-        probs[b, PER_ITEM:PAD_ITEM, :] = jnp.zeros((PAD_ITEM - PER_ITEM, B_DEV), jnp.bfloat16)
-    query_grad = tn_dot(
-        probs[...].reshape(N_GRP * PAD_ITEM, B_DEV), items_all[...].reshape(N_GRP * PAD_ITEM, D)
-    )
-
-    def wait_slabs(j, carry):
-        block_copy(slabs, (g + j) % N_GRP, sib, sl_send_sem, sl_recv_sem, 0).wait_recv()
-        return carry
-
-    lax.fori_loop(1, N_GRP, wait_slabs, 0)
-    weight_sum = slabs[0]
-    for b in range(1, N_GRP):
-        weight_sum = weight_sum + slabs[b]
-    norm = BATCH / weight_sum[:, 0:1]
-    dq_ref[...] = (query_grad * norm).astype(jnp.bfloat16)
-
     pltpu.make_async_copy(recv1.at[pl.ds(0, N_Z - 1)], recv1.at[pl.ds(0, N_Z - 1)], r1_recv_sem).wait()
     turned = jnp.dot(perm[...], recv1[...].reshape(2 * N_Z * N_Y, D), preferred_element_type=jnp.float32)
     send2[...] = turned.astype(jnp.bfloat16).reshape(N_Y, 32, D)
@@ -383,11 +372,22 @@
     lax.fori_loop(1, N_Y, start_rows2, 0)
     recv2[y] = send2[y]
 
+    pltpu.make_async_copy(ids2_recv.at[pl.ds(0, N_Y - 1)], ids2_recv.at[pl.ds(0, N_Y - 1)], i2_recv_sem).wait()
+    got2 = ids2_recv[0]
+    for k in range(1, N_Y):
+        got2 = got2 + ids2_recv[k]
+    in_block = iota((1, D), 1) % 32
+    norm = BATCH / jnp.sum(jnp.where(in_block == 24, got2, 0.0), axis=1, keepdims=True)
+    row_ids = jnp.where(in_block < 2 * N_Z, got2, 0.0).astype(jnp.int32)
+
+    member[...] = jnp.where(iota((ROWS_DEV, D), 0) + 1 == row_ids, 1.0, 0.0).astype(jnp.bfloat16)
+    dq_ref[...] = (query_grad * norm).astype(jnp.bfloat16)
+
+
     for copy in sent:
         copy.wait_send()
     def wait_stats_sent(j, carry):
         stats_copy(j).wait_send()
-        slab_copy(j).wait_send()
         return carry
 
     lax.fori_loop(1, N_GRP, wait_stats_sent, 0)
@@ -418,14 +418,13 @@
             pltpu.VMEM((B_DEV,), bf16),
             pltpu.VMEM((1, PER_ITEM), jnp.int32),
             pltpu.VMEM((1, PER_ITEM), jnp.int32),
-            pltpu.VMEM((N_GRP, 1, 128), f32),
             pltpu.VMEM((N_GRP, PAD_ITEM, D), bf16),
             pltpu.VMEM((N_GRP, B_DEV, D), bf16),
             pltpu.VMEM((N_GRP, PER_ITEM, B_DEV), f32),
             pltpu.VMEM((N_GRP, PAD_ITEM, B_DEV), bf16),
             pltpu.VMEM((N_GRP, PER_ITEM, B_DEV), f32),
             pltpu.VMEM((PER_ITEM, N_GRP * B_DEV), bf16),
-            pltpu.VMEM((N_GRP, 1, 384), f32),
+            pltpu.VMEM((N_GRP, 1, 256), f32),
             pltpu.VMEM((N_Z, 1, 128), f32),
             pltpu.VMEM((N_Z, 1, 128), f32),
             pltpu.VMEM((16, 128), f32),
@@ -438,7 +437,7 @@
             pltpu.VMEM((N_Z, 2 * N_Y, D), bf16),
             pltpu.VMEM((N_Y, 32, D), bf16),
             pltpu.VMEM((N_Y, 32, D), bf16),
-            dma((6,)), dma((N_GRP,)), dma((N_GRP,)),
+            dma((6,)), pltpu.SemaphoreType.REGULAR((3,)), pltpu.SemaphoreType.REGULAR((2,)),
             dma((7,)), dma((N_GRP,)),
             dma((7,)), dma((N_GRP,)),
             dma((N_GRP,)), dma((N_GRP,)),

time: 48.9 us -> 46.5 us (0.951)
  Pallas kernels: 45.9 us -> 43.4 us
    pallas_call x1, Pallas kernels: 45.9 us -> 43.4 us  [shards(): pl.pallas_call(kernel, out_shape=(jax.ShapeDtypeStruct((B_DEV, D), bf16),...]
where the time goes in v3:
time: 46.5 us; the launch traced here: 45.7 us
  Pallas kernels  43.4 us (93%)
  local copies, waits for them, and re-layouts  1.6 us (3%)
  between operations  0.64 us (1%)
    pallas_call x1, Pallas kernels, shards(): pl.pallas_call(kernel, out_shape=(jax.ShapeDtypeStruct((B_DEV, D), bf16),...  43.4 us
    unnamed x2, local copies, waits for them, and re-layouts  1.6 us

profile of v3, /device:TPU:1, one launch (start us, length us, event | category | flops | bytes accessed | tf_op | source)
XLA Modules:
  0.0 45.7 jit_solution(17418705269734653681)
XLA Ops:
  0.6 43.4 %shard_map.77 = (bf16[128,256]{1,0:T(8,128)(2,1)S(1)}, f32[1024,256]{1,0:T(8,128)S(1)}) custom-call(bf16[128,256]{1,0:T(8,128)(2,1)} %q_hbm.1, bf16[160,256]{1,0:T(8,128)(2,1)} %it_hbm.1, bf16[160]{0:T(256)(128)(2,1)} %lq_hbm.1, bf16[128]{0:T(256)(128)(2,1)} %w_hbm.1, s32[1,160]{1,0:T(1,128)} %bitcast.2, s32[1,160]{1,0:T(1,128)} %bitcast.3), custom_call_target="tpu_custom_call" | custom-call | tf_op jit(solution)/shard_map/pallas_call | solution.py:408
  44.1 0.6 %copy.10 = bf16[128,256]{1,0:T(8,128)(2,1)} copy(bf16[128,256]{1,0:T(8,128)(2,1)S(1)} %get-tuple-element.4) | data formatting | bytes 131072
  44.7 1.0 %copy.11 = f32[1024,256]{1,0:T(8,128)} copy(f32[1024,256]{1,0:T(8,128)S(1)} %get-tuple-element.5) | data formatting | bytes 2097152

commit v4 on v3

--- a/solution.py
+++ b/solution.py
@@ -13,7 +13,6 @@
 N_Y = 8
 B_DEV = 128
 PER_ITEM = 160
-PAD_ITEM = 176
 ROWS_DEV = 1024
 D = 256
 BATCH = 98304
@@ -39,11 +38,12 @@
     q_hbm, it_hbm, lq_hbm, w_hbm, own_hbm, row_hbm,
     dq_ref, tab_ref,
     lq_ref, w_ref, own_ref, row_ref,
-    items_all, q_all, logits, probs, cross, grads, stats,
+    items, q_all, w_all, cross, grads, own_stats, stats, dq_keep, dq_send, dq_got, dq_terms, dq_in,
     ids1_send, ids1_recv, ids1_flat, ids2_send, ids2_recv,
     slots, perm, member, send1, recv1, send2, recv2,
     in_sem, z_sems, y_sems,
-    it_send_sem, it_recv_sem, q_send_sem, q_recv_sem, st_send_sem, st_recv_sem,
+    q_send_sem, q_recv_sem, w_send_sem, w_recv_sem, st_send_sem, st_recv_sem,
+    dp_send_sem, dp_recv_sem, dx_send_sem, dx_recv_sem,
     i1_send_sem, i1_recv_sem, i2_send_sem, i2_recv_sem,
     r1_send_sem, r1_recv_sem, r2_send_sem, r2_recv_sem,
 ):
@@ -57,7 +57,7 @@
     loads = [
         pltpu.make_async_copy(src, dst, in_sem.at[i])
         for i, (src, dst) in enumerate((
-            (it_hbm, items_all.at[g, pl.ds(0, PER_ITEM)]),
+            (it_hbm, items),
             (q_hbm, q_all.at[g]),
             (lq_hbm, lq_ref),
             (w_hbm, w_ref),
@@ -93,9 +93,7 @@
         load.wait()
     log_q = lq_ref[...].astype(jnp.float32).reshape(1, PER_ITEM)
     weights = w_ref[...].astype(jnp.float32).reshape(1, B_DEV)
-    padded_lq = jnp.concatenate([log_q, jnp.zeros((1, D - PER_ITEM), jnp.float32)], axis=1)
-    padded_w = jnp.concatenate([weights, jnp.zeros((1, D - B_DEV), jnp.float32)], axis=1)
-    items_all[g, PER_ITEM:PAD_ITEM, :] = jnp.where(iota((16, D), 0) == 0, padded_lq, padded_w).astype(jnp.bfloat16)
+    w_all[g] = weights
 
     pl.semaphore_wait(barrier, (N_GRP - 1) + 2 + 2)
 
@@ -124,7 +122,6 @@
     def arrived(buf, block, sems):
         block_copy(buf, block, sib, sems[0], sems[1], 0).wait_recv()
 
-    it_sems = (it_send_sem, it_recv_sem)
     q_sems = (q_send_sem, q_recv_sem)
 
     def first_sends(buf, sems):
@@ -132,8 +129,16 @@
         send(buf, g, behind_g, sems, 1)
         send(buf, g, sib, sems, 2)
 
-    first_sends(items_all, it_sems)
     first_sends(q_all, q_sems)
+
+    def weights_copy(j):
+        return block_copy(w_all, g, (g + j) % N_GRP, w_send_sem, w_recv_sem, j)
+
+    def start_weights(j, carry):
+        weights_copy(j).start()
+        return carry
+
+    lax.fori_loop(1, N_GRP, start_weights, 0)
     signal_pair(z_sems.at[0], z_peer, 1)
     signal_pair(y_sems.at[0], y_peer, 1)
 
@@ -158,6 +163,7 @@
     right = jnp.where(iota((128, PER_ITEM), 0) == slot_z, 1.0, 0.0).astype(jnp.bfloat16)
     found = nt_dot(left, right)
     ids1 = found[0:16] * 32.0 + found[16:32] + found[32:48]
+
     slots[...] = jnp.where(iota((2 * N_Z * N_Y, PER_ITEM), 0) == slot, 1.0, 0.0).astype(jnp.bfloat16)
     pr, pc = iota((N_Y * 32, 2 * N_Z * N_Y), 0), iota((N_Y * 32, 2 * N_Z * N_Y), 1)
     in_y = pr % 32
@@ -165,59 +171,45 @@
         (in_y < 2 * N_Z) & (pc == (in_y // 2) * (2 * N_Y) + (pr // 32) * 2 + in_y % 2), 1.0, 0.0
     ).astype(jnp.bfloat16)
 
-    ones = jnp.ones((B_DEV, D), jnp.bfloat16)
-    diag = iota((PER_ITEM, D), 0) == iota((PER_ITEM, D), 1)
-
-    def block_logits(block, top):
-        lq = items_all[block, PER_ITEM:PAD_ITEM, :].astype(jnp.float32)[0:1]
-        bias = jnp.where(diag, lq, 0.0).astype(jnp.bfloat16)
-        value = nt_dot(items_all[block, 0:PER_ITEM, :], q_all[g]) - nt_dot(bias, ones)
-        logits[block] = value
-        here = jnp.max(value, axis=0, keepdims=True)
-        return here if top is None else jnp.maximum(top, here)
-
-    def block_cross(block):
-        cross[block] = nt_dot(items_all[g, 0:PER_ITEM, :], q_all[block]) - lq_col
-
-    top = block_logits(g, None)
-    block_cross(g)
-
-    arrived(items_all, behind_g, it_sems)
-    send(items_all, behind_g, ahead_g, it_sems, 3)
-    send(items_all, behind_g, sib, it_sems, 4)
-    arrived(items_all, ahead_g, it_sems)
-    send(items_all, ahead_g, sib, it_sems, 5)
-    pl.semaphore_wait(z_sems.at[0], 2)
-    signal_pair(z_sems.at[1], z_peer, 2)
-    pl.semaphore_wait(y_sems.at[0], 2)
-    signal_pair(y_sems.at[1], y_peer, 2)
+    def block_logits(block):
+        value = nt_dot(items[...], q_all[block]) - lq_col
+        top = jnp.max(value, axis=0, keepdims=True)
+        shifted = jnp.exp(value - top)
+        cross[block] = shifted
+        own_stats[block, :, 0:128] = top
+        own_stats[block, :, 128:256] = jnp.sum(shifted, axis=0, keepdims=True)
+
+    def other_core(chip_x):
+        return 2 * chip_x + 1 - c
+
+    block_logits(g)
+    arrived(q_all, sib, q_sems)
+    block_logits(sib)
     arrived(q_all, behind_g, q_sems)
     send(q_all, behind_g, ahead_g, q_sems, 3)
     send(q_all, behind_g, sib, q_sems, 4)
     arrived(q_all, ahead_g, q_sems)
     send(q_all, ahead_g, sib, q_sems, 5)
-    top = block_logits(behind_g, top)
-    top = block_logits(ahead_g, top)
-    arrived(items_all, far_g, it_sems)
-    send(items_all, far_g, sib, it_sems, 6)
-    top = block_logits(far_g, top)
+    pl.semaphore_wait(z_sems.at[0], 2)
+    signal_pair(z_sems.at[1], z_peer, 2)
+    pl.semaphore_wait(y_sems.at[0], 2)
+    signal_pair(y_sems.at[1], y_peer, 2)
+    block_logits(behind_g)
+    block_logits(ahead_g)
+    arrived(q_all, far_g, q_sems)
+    send(q_all, far_g, sib, q_sems, 6)
+    arrived(q_all, other_core(behind_x), q_sems)
+    block_logits(other_core(behind_x))
+    arrived(q_all, other_core(ahead_x), q_sems)
+    block_logits(other_core(ahead_x))
+    block_logits(far_g)
     pl.semaphore_wait(z_sems.at[1], 2)
     signal_pair(z_sems.at[2], z_peer, 2)
-    arrived(q_all, far_g, q_sems)
-    send(q_all, far_g, sib, q_sems, 6)
-    for other in (x, behind_x, ahead_x, far_x):
-        block = 2 * other + 1 - c
-        arrived(items_all, block, it_sems)
-        top = block_logits(block, top)
-
-    total = jnp.zeros((1, B_DEV), jnp.float32)
+    arrived(q_all, other_core(far_x), q_sems)
+    block_logits(other_core(far_x))
+
     for b in range(N_GRP):
-        shifted = jnp.exp(logits[b] - top)
-        logits[b] = shifted
-        total = total + jnp.sum(shifted, axis=0, keepdims=True)
-
-    stats[g, :, 0:128] = top
-    stats[g, :, 128:256] = 1.0 / total
+        stats[g, b : b + 1, :] = own_stats[b]
 
     def stats_copy(j):
         return block_copy(stats, g, (g + j) % N_GRP, st_send_sem, st_recv_sem, j)
@@ -228,20 +220,22 @@
 
     lax.fori_loop(1, N_GRP, start_stats, 0)
 
-    def block_weights(block):
-        return items_all[block, PER_ITEM:PAD_ITEM, 0:B_DEV].astype(jnp.float32)[1:2]
-
-    group_sum = jnp.zeros((1, 1), jnp.float32)
-    for b in range(N_GRP):
-        group_sum = group_sum + jnp.sum(block_weights(b), axis=1, keepdims=True)
+    def wait_weights(j, carry):
+        block_copy(w_all, (g + j) % N_GRP, sib, w_send_sem, w_recv_sem, 0).wait_recv()
+        return carry
+
+    lax.fori_loop(1, N_GRP, wait_weights, 0)
+    all_weights = w_all[0]
+    for b in range(1, N_GRP):
+        all_weights = all_weights + w_all[b]
+    group_sum = jnp.sum(all_weights, axis=1, keepdims=True)
     ids1 = jnp.where(iota((16, 128), 1) == 2 * N_Y, group_sum, ids1)
     for k in range(N_Z):
         ids1_send[k] = ids1[k : k + 1]
     ids1_recv[z] = ids1_send[z]
 
-
+    pl.semaphore_wait(y_sems.at[1], 2)
     pl.semaphore_wait(z_sems.at[2], 2)
-    pl.semaphore_wait(y_sems.at[1], 2)
 
     def ids1_copy(j):
         zt = (z + j) % N_Z
@@ -260,25 +254,23 @@
 
     lax.fori_loop(1, N_Z, start_ids1, 0)
 
-    block_cross(behind_g)
-    block_cross(ahead_g)
-    block_cross(far_g)
-    for other in (x, behind_x, ahead_x, far_x):
-        block = 2 * other + 1 - c
-        arrived(q_all, block, q_sems)
-        block_cross(block)
-
     def wait_stats(j, carry):
         block_copy(stats, (g + j) % N_GRP, sib, st_send_sem, st_recv_sem, 0).wait_recv()
         return carry
 
     lax.fori_loop(1, N_GRP, wait_stats, 0)
 
+    tops = [stats[b, :, 0:128] for b in range(N_GRP)]
+    top = functools.reduce(jnp.maximum, tops)
+    total = jnp.zeros((N_GRP, B_DEV), jnp.float32)
+    for b in range(N_GRP):
+        total = total + jnp.exp(tops[b] - top) * stats[b, :, 128:256]
+    scale = jnp.exp(stats[g, :, 0:128] - top) / total
     pos_sub, pos_lane = iota((PER_ITEM, B_DEV), 0), iota((PER_ITEM, B_DEV), 1)
     for b in range(N_GRP):
-        share = jnp.exp(cross[b] - stats[b, :, 0:128]) * stats[b, :, 128:256]
+        share = cross[b] * scale[b : b + 1]
         share = share - jnp.where(pos_sub + b * PER_ITEM == pos_lane + g * PER_ITEM, 1.0, 0.0)
-        grads[:, b * B_DEV : (b + 1) * B_DEV] = (block_weights(b) * share).astype(jnp.bfloat16)
+        grads[:, b * B_DEV : (b + 1) * B_DEV] = (w_all[b] * share).astype(jnp.bfloat16)
     item_grad = jnp.dot(
         grads[...], q_all[...].reshape(N_GRP * B_DEV, D), preferred_element_type=jnp.float32
     ).astype(jnp.bfloat16)
@@ -303,15 +295,25 @@
     lax.fori_loop(1, N_Z, start_rows1, 0)
     recv1[z] = send1[z]
 
-    inverse = 1.0 / total
-    for b in range(N_GRP):
-        share = logits[b] * inverse
-        share = share - jnp.where(pos_sub + b * PER_ITEM == pos_lane + g * PER_ITEM, 1.0, 0.0)
-        probs[b, 0:PER_ITEM, :] = (weights * share).astype(jnp.bfloat16)
-        probs[b, PER_ITEM:PAD_ITEM, :] = jnp.zeros((PAD_ITEM - PER_ITEM, B_DEV), jnp.bfloat16)
-    query_grad = tn_dot(
-        probs[...].reshape(N_GRP * PAD_ITEM, B_DEV), items_all[...].reshape(N_GRP * PAD_ITEM, D)
-    )
+    def query_term(block):
+        columns = pl.ds(pl.multiple_of(block * B_DEV, B_DEV), B_DEV)
+        return tn_dot(grads[:, columns], items[...])
+
+    def pair_copy(k):
+        return pltpu.make_async_remote_copy(
+            src_ref=dq_send.at[k],
+            dst_ref=dq_got.at[k],
+            send_sem=dp_send_sem.at[k],
+            recv_sem=dp_recv_sem.at[k],
+            device_id={"grp": sib},
+            device_id_type=MESH,
+        )
+
+    for k in range(N_X):
+        dq_send[k] = query_term(2 * chip(k) + 1 - c)
+        pair_copy(k).start()
+    for k in range(N_X):
+        dq_keep[k] = query_term(2 * chip(k) + c)
 
     pltpu.make_async_copy(ids1_recv.at[pl.ds(0, N_Z - 1)], ids1_recv.at[pl.ds(0, N_Z - 1)], i1_recv_sem).wait()
     ids1_flat[...] = jnp.zeros((16, 128), jnp.float32)
@@ -350,6 +352,22 @@
 
     lax.fori_loop(1, N_Y, start_ids2, 0)
 
+    def chip_copy(k):
+        return pltpu.make_async_remote_copy(
+            src_ref=dq_terms.at[k],
+            dst_ref=dq_in.at[k],
+            send_sem=dx_send_sem.at[k],
+            recv_sem=dx_recv_sem.at[k],
+            device_id={"grp": 2 * chip(k) + c},
+            device_id_type=MESH,
+        )
+
+    for k in (2, 1, 3):
+        pair_copy(k).wait_recv()
+        dq_terms[k] = (dq_keep[k] + dq_got[k]).astype(jnp.bfloat16)
+        chip_copy(k).start()
+    pair_copy(0).wait_recv()
+
     pltpu.make_async_copy(recv1.at[pl.ds(0, N_Z - 1)], recv1.at[pl.ds(0, N_Z - 1)], r1_recv_sem).wait()
     turned = jnp.dot(perm[...], recv1[...].reshape(2 * N_Z * N_Y, D), preferred_element_type=jnp.float32)
     send2[...] = turned.astype(jnp.bfloat16).reshape(N_Y, 32, D)
@@ -381,13 +399,22 @@
     row_ids = jnp.where(in_block < 2 * N_Z, got2, 0.0).astype(jnp.int32)
 
     member[...] = jnp.where(iota((ROWS_DEV, D), 0) + 1 == row_ids, 1.0, 0.0).astype(jnp.bfloat16)
+    query_grad = dq_keep[0] + dq_got[0]
+    for k in (1, 3, 2):
+        chip_copy(k).wait_recv()
+        query_grad = query_grad + dq_in[k].astype(jnp.float32)
     dq_ref[...] = (query_grad * norm).astype(jnp.bfloat16)
 
 
     for copy in sent:
         copy.wait_send()
+    for k in range(N_X):
+        pair_copy(k).wait_send()
+    for k in range(1, N_X):
+        chip_copy(k).wait_send()
     def wait_stats_sent(j, carry):
         stats_copy(j).wait_send()
+        weights_copy(j).wait_send()
         return carry
 
     lax.fori_loop(1, N_GRP, wait_stats_sent, 0)
@@ -418,13 +445,18 @@
             pltpu.VMEM((B_DEV,), bf16),
             pltpu.VMEM((1, PER_ITEM), jnp.int32),
             pltpu.VMEM((1, PER_ITEM), jnp.int32),
-            pltpu.VMEM((N_GRP, PAD_ITEM, D), bf16),
+            pltpu.VMEM((PER_ITEM, D), bf16),
             pltpu.VMEM((N_GRP, B_DEV, D), bf16),
-            pltpu.VMEM((N_GRP, PER_ITEM, B_DEV), f32),
-            pltpu.VMEM((N_GRP, PAD_ITEM, B_DEV), bf16),
+            pltpu.VMEM((N_GRP, 1, B_DEV), f32),
             pltpu.VMEM((N_GRP, PER_ITEM, B_DEV), f32),
             pltpu.VMEM((PER_ITEM, N_GRP * B_DEV), bf16),
             pltpu.VMEM((N_GRP, 1, 256), f32),
+            pltpu.VMEM((N_GRP, N_GRP, 256), f32),
+            pltpu.VMEM((N_X, B_DEV, D), f32),
+            pltpu.VMEM((N_X, B_DEV, D), f32),
+            pltpu.VMEM((N_X, B_DEV, D), f32),
+            pltpu.VMEM((N_X, B_DEV, D), bf16),
+            pltpu.VMEM((N_X, B_DEV, D), bf16),
             pltpu.VMEM((N_Z, 1, 128), f32),
             pltpu.VMEM((N_Z, 1, 128), f32),
             pltpu.VMEM((16, 128), f32),
@@ -439,8 +471,9 @@
             pltpu.VMEM((N_Y, 32, D), bf16),
             dma((6,)), pltpu.SemaphoreType.REGULAR((3,)), pltpu.SemaphoreType.REGULAR((2,)),
             dma((7,)), dma((N_GRP,)),
-            dma((7,)), dma((N_GRP,)),
             dma((N_GRP,)), dma((N_GRP,)),
+            dma((N_GRP,)), dma((N_GRP,)),
+            dma((N_X,)), dma((N_X,)), dma((N_X,)), dma((N_X,)),
             dma, dma, dma, dma, dma, dma, dma, dma,
         ],
         compiler_params=pltpu.CompilerParams(

time: 46.5 us -> 44.8 us (0.963); the launches traced: 45.7 us -> 44.6 us
  Pallas kernels: 43.4 us -> 42.4 us
    pallas_call x1, Pallas kernels: 43.4 us -> 42.4 us  [shards(): pl.pallas_call(kernel, out_shape=(jax.ShapeDtypeStruct((B_DEV, D), bf16),...]
where the time goes in v4:
time: 44.8 us; the launch traced here: 44.6 us
  Pallas kernels  42.4 us (95%)
  local copies, waits for them, and re-layouts  1.6 us (4%)
  between operations  0.64 us (1%)
    pallas_call x1, Pallas kernels, shards(): pl.pallas_call(kernel, out_shape=(jax.ShapeDtypeStruct((B_DEV, D), bf16),...  42.4 us
    unnamed x2, local copies, waits for them, and re-layouts  1.6 us

profile of v4, /device:TPU:1, one launch (start us, length us, event | category | flops | bytes accessed | tf_op | source)
XLA Modules:
  0.0 44.6 jit_solution(2071401698654655566)
XLA Ops:
  0.6 42.4 %shard_map.77 = (bf16[128,256]{1,0:T(8,128)(2,1)S(1)}, f32[1024,256]{1,0:T(8,128)S(1)}) custom-call(bf16[128,256]{1,0:T(8,128)(2,1)} %q_hbm.1, bf16[160,256]{1,0:T(8,128)(2,1)} %it_hbm.1, bf16[160]{0:T(256)(128)(2,1)} %lq_hbm.1, bf16[128]{0:T(256)(128)(2,1)} %w_hbm.1, s32[1,160]{1,0:T(1,128)} %bitcast.2, s32[1,160]{1,0:T(1,128)} %bitcast.3), custom_call_target="tpu_custom_call" | custom-call | tf_op jit(solution)/shard_map/pallas_call | solution.py:435
  43.0 0.6 %copy.10 = bf16[128,256]{1,0:T(8,128)(2,1)} copy(bf16[128,256]{1,0:T(8,128)(2,1)S(1)} %get-tuple-element.4) | data formatting | bytes 131072
  43.7 1.0 %copy.11 = f32[1024,256]{1,0:T(8,128)} copy(f32[1024,256]{1,0:T(8,128)S(1)} %get-tuple-element.5) | data formatting | bytes 2097152

commit v5 on v4

--- a/solution.py
+++ b/solution.py
@@ -12,10 +12,13 @@
 N_Z = 12
 N_Y = 8
 B_DEV = 128
+Q_ROWS = 144
 PER_ITEM = 160
 ROWS_DEV = 1024
 D = 256
 BATCH = 98304
+Z_ORDER = (6, 5, 7, 4, 8, 3, 9, 2, 10, 1, 11)
+Y_ORDER = (4, 3, 5, 2, 6, 1, 7)
 MESH = pl.DeviceIdType.MESH
 HIGHEST = lax.Precision.HIGHEST
 
@@ -38,11 +41,11 @@
     q_hbm, it_hbm, lq_hbm, w_hbm, own_hbm, row_hbm,
     dq_ref, tab_ref,
     lq_ref, w_ref, own_ref, row_ref,
-    items, q_all, w_all, cross, grads, own_stats, stats, dq_keep, dq_send, dq_got, dq_terms, dq_in,
+    items, q_all, cross, grads, own_stats, stats, dq_keep, dq_send, dq_got, dq_terms, dq_in,
     ids1_send, ids1_recv, ids1_flat, ids2_send, ids2_recv,
     slots, perm, member, send1, recv1, send2, recv2,
     in_sem, z_sems, y_sems,
-    q_send_sem, q_recv_sem, w_send_sem, w_recv_sem, st_send_sem, st_recv_sem,
+    q_send_sem, q_recv_sem, st_send_sem, st_recv_sem,
     dp_send_sem, dp_recv_sem, dx_send_sem, dx_recv_sem,
     i1_send_sem, i1_recv_sem, i2_send_sem, i2_recv_sem,
     r1_send_sem, r1_recv_sem, r2_send_sem, r2_recv_sem,
@@ -58,7 +61,7 @@
         pltpu.make_async_copy(src, dst, in_sem.at[i])
         for i, (src, dst) in enumerate((
             (it_hbm, items),
-            (q_hbm, q_all.at[g]),
+            (q_hbm, q_all.at[g, pl.ds(0, B_DEV)]),
             (lq_hbm, lq_ref),
             (w_hbm, w_ref),
             (own_hbm, own_ref),
@@ -70,11 +73,13 @@
 
     barrier = pltpu.get_barrier_semaphore()
 
-    def greet_grp(j, carry):
-        pl.semaphore_signal(barrier, inc=1, device_id={"grp": (g + j) % N_GRP}, device_id_type=MESH)
-        return carry
-
-    lax.fori_loop(1, N_GRP, greet_grp, 0)
+    def chip(dx):
+        return (x + dx + N_X) % N_X
+
+    behind_x, ahead_x, far_x = chip(-ahead), chip(ahead), chip(2)
+    behind_g, ahead_g, far_g = 2 * behind_x + c, 2 * ahead_x + c, 2 * far_x + c
+    for peer in (ahead_g, behind_g, sib, far_g):
+        pl.semaphore_signal(barrier, inc=1, device_id={"grp": peer}, device_id_type=MESH)
 
     def z_peer(step):
         return {"dp": ((z + step + N_Z) % N_Z) * N_Y + y}
@@ -93,9 +98,10 @@
         load.wait()
     log_q = lq_ref[...].astype(jnp.float32).reshape(1, PER_ITEM)
     weights = w_ref[...].astype(jnp.float32).reshape(1, B_DEV)
-    w_all[g] = weights
-
-    pl.semaphore_wait(barrier, (N_GRP - 1) + 2 + 2)
+    padded_w = jnp.concatenate([weights, jnp.zeros((1, D - B_DEV), jnp.float32)], axis=1)
+    q_all[g, B_DEV:Q_ROWS, :] = jnp.broadcast_to(padded_w, (Q_ROWS - B_DEV, D)).astype(jnp.bfloat16)
+
+    pl.semaphore_wait(barrier, 4 + 2 + 2)
 
     def block_copy(buf, block, target, send_sem, recv_sem, index):
         return pltpu.make_async_remote_copy(
@@ -107,11 +113,6 @@
             device_id_type=MESH,
         )
 
-    def chip(dx):
-        return (x + dx + N_X) % N_X
-
-    behind_x, ahead_x, far_x = chip(-ahead), chip(ahead), chip(2)
-    behind_g, ahead_g, far_g = 2 * behind_x + c, 2 * ahead_x + c, 2 * far_x + c
     sent = []
 
     def send(buf, block, target, sems, index):
@@ -125,20 +126,13 @@
     q_sems = (q_send_sem, q_recv_sem)
 
     def first_sends(buf, sems):
+        send(buf, g, far_g, sems, 3)
         send(buf, g, ahead_g, sems, 0)
         send(buf, g, behind_g, sems, 1)
         send(buf, g, sib, sems, 2)
 
     first_sends(q_all, q_sems)
 
-    def weights_copy(j):
-        return block_copy(w_all, g, (g + j) % N_GRP, w_send_sem, w_recv_sem, j)
-
-    def start_weights(j, carry):
-        weights_copy(j).start()
-        return carry
-
-    lax.fori_loop(1, N_GRP, start_weights, 0)
     signal_pair(z_sems.at[0], z_peer, 1)
     signal_pair(y_sems.at[0], y_peer, 1)
 
@@ -172,7 +166,7 @@
     ).astype(jnp.bfloat16)
 
     def block_logits(block):
-        value = nt_dot(items[...], q_all[block]) - lq_col
+        value = nt_dot(items[...], q_all[block, 0:B_DEV, :]) - lq_col
         top = jnp.max(value, axis=0, keepdims=True)
         shifted = jnp.exp(value - top)
         cross[block] = shifted
@@ -186,7 +180,6 @@
     arrived(q_all, sib, q_sems)
     block_logits(sib)
     arrived(q_all, behind_g, q_sems)
-    send(q_all, behind_g, ahead_g, q_sems, 3)
     send(q_all, behind_g, sib, q_sems, 4)
     arrived(q_all, ahead_g, q_sems)
     send(q_all, ahead_g, sib, q_sems, 5)
@@ -211,23 +204,20 @@
     for b in range(N_GRP):
         stats[g, b : b + 1, :] = own_stats[b]
 
+    others = (
+        far_g, other_core(far_x), ahead_g, behind_g, other_core(ahead_x), other_core(behind_x), sib
+    )
+
     def stats_copy(j):
-        return block_copy(stats, g, (g + j) % N_GRP, st_send_sem, st_recv_sem, j)
-
-    def start_stats(j, carry):
+        return block_copy(stats, g, others[j], st_send_sem, st_recv_sem, j)
+
+    for j in range(N_GRP - 1):
         stats_copy(j).start()
-        return carry
-
-    lax.fori_loop(1, N_GRP, start_stats, 0)
-
-    def wait_weights(j, carry):
-        block_copy(w_all, (g + j) % N_GRP, sib, w_send_sem, w_recv_sem, 0).wait_recv()
-        return carry
-
-    lax.fori_loop(1, N_GRP, wait_weights, 0)
-    all_weights = w_all[0]
+
+    block_weights = [q_all[b, B_DEV:Q_ROWS, 0:B_DEV].astype(jnp.float32)[0:1] for b in range(N_GRP)]
+    all_weights = block_weights[0]
     for b in range(1, N_GRP):
-        all_weights = all_weights + w_all[b]
+        all_weights = all_weights + block_weights[b]
     group_sum = jnp.sum(all_weights, axis=1, keepdims=True)
     ids1 = jnp.where(iota((16, 128), 1) == 2 * N_Y, group_sum, ids1)
     for k in range(N_Z):
@@ -238,7 +228,7 @@
     pl.semaphore_wait(z_sems.at[2], 2)
 
     def ids1_copy(j):
-        zt = (z + j) % N_Z
+        zt = jnp.where(z + j >= N_Z, z + j - N_Z, z + j)
         return pltpu.make_async_remote_copy(
             src_ref=ids1_send.at[zt],
             dst_ref=ids1_recv.at[z],
@@ -248,17 +238,11 @@
             device_id_type=MESH,
         )
 
-    def start_ids1(j, carry):
+    for j in Z_ORDER:
         ids1_copy(j).start()
-        return carry
-
-    lax.fori_loop(1, N_Z, start_ids1, 0)
-
-    def wait_stats(j, carry):
-        block_copy(stats, (g + j) % N_GRP, sib, st_send_sem, st_recv_sem, 0).wait_recv()
-        return carry
-
-    lax.fori_loop(1, N_GRP, wait_stats, 0)
+
+    for other in others:
+        block_copy(stats, other, sib, st_send_sem, st_recv_sem, 0).wait_recv()
 
     tops = [stats[b, :, 0:128] for b in range(N_GRP)]
     top = functools.reduce(jnp.maximum, tops)
@@ -270,15 +254,15 @@
     for b in range(N_GRP):
         share = cross[b] * scale[b : b + 1]
         share = share - jnp.where(pos_sub + b * PER_ITEM == pos_lane + g * PER_ITEM, 1.0, 0.0)
-        grads[:, b * B_DEV : (b + 1) * B_DEV] = (w_all[b] * share).astype(jnp.bfloat16)
+        grads[:, b * B_DEV : (b + 1) * B_DEV] = (block_weights[b] * share).astype(jnp.bfloat16)
     item_grad = jnp.dot(
-        grads[...], q_all[...].reshape(N_GRP * B_DEV, D), preferred_element_type=jnp.float32
+        grads[...], q_all[:, 0:B_DEV, :].reshape(N_GRP * B_DEV, D), preferred_element_type=jnp.float32
     ).astype(jnp.bfloat16)
     placed = jnp.dot(slots[...], item_grad, preferred_element_type=jnp.float32)
     send1[...] = placed.astype(jnp.bfloat16).reshape(N_Z, 2 * N_Y, D)
 
     def rows1_copy(j):
-        zt = (z + j) % N_Z
+        zt = jnp.where(z + j >= N_Z, z + j - N_Z, z + j)
         return pltpu.make_async_remote_copy(
             src_ref=send1.at[zt],
             dst_ref=recv1.at[z],
@@ -288,11 +272,8 @@
             device_id_type=MESH,
         )
 
-    def start_rows1(j, carry):
+    for j in Z_ORDER:
         rows1_copy(j).start()
-        return carry
-
-    lax.fori_loop(1, N_Z, start_rows1, 0)
     recv1[z] = send1[z]
 
     def query_term(block):
@@ -336,7 +317,7 @@
     ids2_recv[y] = ids2_send[y]
 
     def ids2_copy(j):
-        yt = (y + j) % N_Y
+        yt = jnp.where(y + j >= N_Y, y + j - N_Y, y + j)
         return pltpu.make_async_remote_copy(
             src_ref=ids2_send.at[yt],
             dst_ref=ids2_recv.at[y],
@@ -346,11 +327,8 @@
             device_id_type=MESH,
         )
 
-    def start_ids2(j, carry):
+    for j in Y_ORDER:
         ids2_copy(j).start()
-        return carry
-
-    lax.fori_loop(1, N_Y, start_ids2, 0)
 
     def chip_copy(k):
         return pltpu.make_async_remote_copy(
@@ -373,7 +351,7 @@
     send2[...] = turned.astype(jnp.bfloat16).reshape(N_Y, 32, D)
 
     def rows2_copy(j):
-        yt = (y + j) % N_Y
+        yt = jnp.where(y + j >= N_Y, y + j - N_Y, y + j)
         return pltpu.make_async_remote_copy(
             src_ref=send2.at[yt],
             dst_ref=recv2.at[y],
@@ -383,11 +361,8 @@
             device_id_type=MESH,
         )
 
-    def start_rows2(j, carry):
+    for j in Y_ORDER:
         rows2_copy(j).start()
-        return carry
-
-    lax.fori_loop(1, N_Y, start_rows2, 0)
     recv2[y] = send2[y]
 
     pltpu.make_async_copy(ids2_recv.at[pl.ds(0, N_Y - 1)], ids2_recv.at[pl.ds(0, N_Y - 1)], i2_recv_sem).wait()
@@ -412,12 +387,8 @@
         pair_copy(k).wait_send()
     for k in range(1, N_X):
         chip_copy(k).wait_send()
-    def wait_stats_sent(j, carry):
+    for j in range(N_GRP - 1):
         stats_copy(j).wait_send()
-        weights_copy(j).wait_send()
-        return carry
-
-    lax.fori_loop(1, N_GRP, wait_stats_sent, 0)
     pltpu.make_async_copy(ids1_send.at[pl.ds(0, N_Z - 1)], ids1_send.at[pl.ds(0, N_Z - 1)], i1_send_sem).wait()
     pltpu.make_async_copy(ids2_send.at[pl.ds(0, N_Y - 1)], ids2_send.at[pl.ds(0, N_Y - 1)], i2_send_sem).wait()
     pltpu.make_async_copy(send1.at[pl.ds(0, N_Z - 1)], send1.at[pl.ds(0, N_Z - 1)], r1_send_sem).wait()
@@ -446,8 +417,7 @@
             pltpu.VMEM((1, PER_ITEM), jnp.int32),
             pltpu.VMEM((1, PER_ITEM), jnp.int32),
             pltpu.VMEM((PER_ITEM, D), bf16),
-            pltpu.VMEM((N_GRP, B_DEV, D), bf16),
-            pltpu.VMEM((N_GRP, 1, B_DEV), f32),
+            pltpu.VMEM((N_GRP, Q_ROWS, D), bf16),
             pltpu.VMEM((N_GRP, PER_ITEM, B_DEV), f32),
             pltpu.VMEM((PER_ITEM, N_GRP * B_DEV), bf16),
             pltpu.VMEM((N_GRP, 1, 256), f32),
@@ -472,7 +442,6 @@
             dma((6,)), pltpu.SemaphoreType.REGULAR((3,)), pltpu.SemaphoreType.REGULAR((2,)),
             dma((7,)), dma((N_GRP,)),
             dma((N_GRP,)), dma((N_GRP,)),
-            dma((N_GRP,)), dma((N_GRP,)),
             dma((N_X,)), dma((N_X,)), dma((N_X,)), dma((N_X,)),
             dma, dma, dma, dma, dma, dma, dma, dma,
         ],

time: 44.8 us -> 42.6 us (0.951)
  Pallas kernels: 42.4 us -> 40.1 us
    pallas_call x1, Pallas kernels: 42.4 us -> 40.1 us  [shards(): pl.pallas_call(kernel, out_shape=(jax.ShapeDtypeStruct((B_DEV, D), bf16),...]
where the time goes in v5:
time: 42.6 us; the launch traced here: 42.3 us
  Pallas kernels  40.1 us (94%)
  local copies, waits for them, and re-layouts  1.6 us (4%)
  between operations  0.64 us (2%)
    pallas_call x1, Pallas kernels, shards(): pl.pallas_call(kernel, out_shape=(jax.ShapeDtypeStruct((B_DEV, D), bf16),...  40.1 us
    unnamed x2, local copies, waits for them, and re-layouts  1.6 us

profile of v5, /device:TPU:1, one launch (start us, length us, event | category | flops | bytes accessed | tf_op | source)
XLA Modules:
  0.0 42.3 jit_solution(5998368420485671344)
XLA Ops:
  0.6 40.1 %shard_map.77 = (bf16[128,256]{1,0:T(8,128)(2,1)S(1)}, f32[1024,256]{1,0:T(8,128)S(1)}) custom-call(bf16[128,256]{1,0:T(8,128)(2,1)} %q_hbm.1, bf16[160,256]{1,0:T(8,128)(2,1)} %it_hbm.1, bf16[160]{0:T(256)(128)(2,1)} %lq_hbm.1, bf16[128]{0:T(256)(128)(2,1)} %w_hbm.1, s32[1,160]{1,0:T(1,128)} %bitcast.2, s32[1,160]{1,0:T(1,128)} %bitcast.3), custom_call_target="tpu_custom_call" | custom-call | tf_op jit(solution)/shard_map/pallas_call | solution.py:406
  40.7 0.6 %copy.10 = bf16[128,256]{1,0:T(8,128)(2,1)} copy(bf16[128,256]{1,0:T(8,128)(2,1)S(1)} %get-tuple-element.4) | data formatting | bytes 131072
  41.4 1.0 %copy.11 = f32[1024,256]{1,0:T(8,128)} copy(f32[1024,256]{1,0:T(8,128)S(1)} %get-tuple-element.5) | data formatting | bytes 2097152

commit v6 on v5

--- a/solution.py
+++ b/solution.py
@@ -17,6 +17,7 @@
 ROWS_DEV = 1024
 D = 256
 BATCH = 98304
+CHUNKS = 4
 Z_ORDER = (6, 5, 7, 4, 8, 3, 9, 2, 10, 1, 11)
 Y_ORDER = (4, 3, 5, 2, 6, 1, 7)
 MESH = pl.DeviceIdType.MESH
@@ -39,11 +40,11 @@
 
 def kernel(
     q_hbm, it_hbm, lq_hbm, w_hbm, own_hbm, row_hbm,
-    dq_ref, tab_ref,
+    dq_ref, rows_ref, member, norm_ref,
     lq_ref, w_ref, own_ref, row_ref,
     items, q_all, cross, grads, own_stats, stats, dq_keep, dq_send, dq_got, dq_terms, dq_in,
     ids1_send, ids1_recv, ids1_flat, ids2_send, ids2_recv,
-    slots, perm, member, send1, recv1, send2, recv2,
+    slots, perm, send1, recv1, send2, recv2,
     in_sem, z_sems, y_sems,
     q_send_sem, q_recv_sem, st_send_sem, st_recv_sem,
     dp_send_sem, dp_recv_sem, dx_send_sem, dx_recv_sem,
@@ -393,24 +394,45 @@
     pltpu.make_async_copy(ids2_send.at[pl.ds(0, N_Y - 1)], ids2_send.at[pl.ds(0, N_Y - 1)], i2_send_sem).wait()
     pltpu.make_async_copy(send1.at[pl.ds(0, N_Z - 1)], send1.at[pl.ds(0, N_Z - 1)], r1_send_sem).wait()
     pltpu.make_async_copy(recv2.at[pl.ds(0, N_Y - 1)], recv2.at[pl.ds(0, N_Y - 1)], r2_recv_sem).wait()
-    tab_ref[...] = norm * jnp.dot(
-        member[...], recv2[...].reshape(N_Y * 32, D), preferred_element_type=jnp.float32
-    )
+    rows_ref[...] = recv2[...].reshape(N_Y * 32, D)
+    norm_ref[...] = jnp.broadcast_to(norm, (1, D))
     pltpu.make_async_copy(send2.at[pl.ds(0, N_Y - 1)], send2.at[pl.ds(0, N_Y - 1)], r2_send_sem).wait()
+
+
+def write_out(query_ref, rows_ref, member_ref, norm_ref, dq_out, tab_out, table, dq_sem, tab_sems):
+    query_copy = pltpu.make_async_copy(query_ref, dq_out, dq_sem)
+    query_copy.start()
+    size = ROWS_DEV // CHUNKS
+    copies = []
+    for k in range(CHUNKS):
+        part = slice(k * size, (k + 1) * size)
+        table[part, :] = norm_ref[...] * jnp.dot(
+            member_ref[part, :], rows_ref[...], preferred_element_type=jnp.float32
+        )
+        copy = pltpu.make_async_copy(
+            table.at[pl.ds(k * size, size)], tab_out.at[pl.ds(k * size, size)], tab_sems.at[k]
+        )
+        copy.start()
+        copies.append(copy)
+    query_copy.wait()
+    for copy in copies:
+        copy.wait()
 
 
 def shards(queries, item_vecs, log_q, weights, item_owner, item_row):
     vmem = pl.BlockSpec(memory_space=pltpu.VMEM)
     bf16, f32 = jnp.bfloat16, jnp.float32
     dma = pltpu.SemaphoreType.DMA
-    return pl.pallas_call(
+    query_grad, rows, member, norm = pl.pallas_call(
         kernel,
         out_shape=(
             jax.ShapeDtypeStruct((B_DEV, D), bf16),
-            jax.ShapeDtypeStruct((ROWS_DEV, D), f32),
+            jax.ShapeDtypeStruct((N_Y * 32, D), bf16),
+            jax.ShapeDtypeStruct((ROWS_DEV, D), bf16),
+            jax.ShapeDtypeStruct((1, D), f32),
         ),
         in_specs=[pl.BlockSpec(memory_space=pltpu.HBM)] * 6,
-        out_specs=(vmem, vmem),
+        out_specs=(vmem,) * 4,
         scratch_shapes=[
             pltpu.VMEM((PER_ITEM,), bf16),
             pltpu.VMEM((B_DEV,), bf16),
@@ -434,7 +456,6 @@
             pltpu.VMEM((N_Y, 1, D), f32),
             pltpu.VMEM((2 * N_Z * N_Y, PER_ITEM), bf16),
             pltpu.VMEM((N_Y * 32, 2 * N_Z * N_Y), bf16),
-            pltpu.VMEM((ROWS_DEV, D), bf16),
             pltpu.VMEM((N_Z, 2 * N_Y, D), bf16),
             pltpu.VMEM((N_Z, 2 * N_Y, D), bf16),
             pltpu.VMEM((N_Y, 32, D), bf16),
@@ -459,6 +480,18 @@
             item_row.reshape(1, PER_ITEM),
         )
     ))
+    hbm = pl.BlockSpec(memory_space=pl.ANY)
+    return pl.pallas_call(
+        write_out,
+        out_shape=(
+            jax.ShapeDtypeStruct((B_DEV, D), bf16),
+            jax.ShapeDtypeStruct((ROWS_DEV, D), f32),
+        ),
+        in_specs=[vmem] * 4,
+        out_specs=(hbm, hbm),
+        scratch_shapes=[pltpu.VMEM((ROWS_DEV, D), f32), dma, dma((CHUNKS,))],
+        compiler_params=pltpu.CompilerParams(vmem_limit_bytes=32 * 1024 * 1024),
+    )(query_grad, rows, member, norm)
 
 
 def solution(mesh):

time: 42.6 us -> 41.9 us (0.984)
  local copies, waits for them, and re-layouts: 1.6 us -> 0 us
  Pallas kernels: 40.1 us -> 41 us
    unnamed x2 -> x0, local copies, waits for them, and re-layouts: 1.6 us -> none
    pallas_call x0 -> x1, Pallas kernels: none -> 1.24 us  [shards(): pl.pallas_call(write_out, out_shape=(jax.ShapeDtypeStruct((B_DEV, D), bf1...]
where the time goes in v6:
time: 41.9 us; the launch traced here: 41.7 us
  Pallas kernels  41 us (98%)
  between operations  0.64 us (2%)
    pallas_call x1, Pallas kernels, shards(): pl.pallas_call(kernel, out_shape=(jax.ShapeDtypeStruct((B_DEV, D), bf16),...  39.8 us
    pallas_call x1, Pallas kernels, shards(): pl.pallas_call(write_out, out_shape=(jax.ShapeDtypeStruct((B_DEV, D), bf1...  1.24 us

profile of v6, /device:TPU:1, one launch (start us, length us, event | category | flops | bytes accessed | tf_op | source)
XLA Modules:
  0.0 41.7 jit_solution(1982151639049469600)
XLA Ops:
  0.6 39.8 %shard_map.77 = (bf16[128,256]{1,0:T(8,128)(2,1)S(1)}, bf16[256,256]{1,0:T(8,128)(2,1)S(1)}, bf16[1024,256]{1,0:T(8,128)(2,1)S(1)}, f32[1,256]{1,0:T(1,128)S(1)}) custom-call(bf16[128,256]{1,0:T(8,128)(2,1)} %q_hbm.1, bf16[160,256]{1,0:T(8,128)(2,1)} %it_hbm.1, bf16[160]{0:T(256)(128)(2,1)} %lq_hbm.1, bf16[128]{0:T(256)(128)(2,1)} %w_hbm.1, ...), custom_call_target="tpu_custom_call" | custom-call | tf_op jit(solution)/shard_map/pallas_call | solution.py:426
  40.4 1.2 %shard_map.78 = (bf16[128,256]{1,0:T(8,128)(2,1)}, f32[1024,256]{1,0:T(8,128)}) custom-call(bf16[128,256]{1,0:T(8,128)(2,1)S(1)} %get-tuple-element.6.query_ref, bf16[256,256]{1,0:T(8,128)(2,1)S(1)} %get-tuple-element.7.rows_ref, bf16[1024,256]{1,0:T(8,128)(2,1)S(1)} %get-tuple-element.8.member_ref, f32[1,256]{1,0:T(1,128)S(1)} %get-tuple-element.9.norm_ref), custom_call_target="tpu_custom_call" | custom-call | tf_op jit(solution)/shard_map/pallas_call | solution.py:484

commit v7 on v6

--- a/solution.py
+++ b/solution.py
@@ -45,7 +45,7 @@
     items, q_all, cross, grads, own_stats, stats, dq_keep, dq_send, dq_got, dq_terms, dq_in,
     ids1_send, ids1_recv, ids1_flat, ids2_send, ids2_recv,
     slots, perm, send1, recv1, send2, recv2,
-    in_sem, z_sems, y_sems,
+    in_sem, z_sems, y_sem,
     q_send_sem, q_recv_sem, st_send_sem, st_recv_sem,
     dp_send_sem, dp_recv_sem, dx_send_sem, dx_recv_sem,
     i1_send_sem, i1_recv_sem, i2_send_sem, i2_recv_sem,
@@ -92,8 +92,9 @@
         pl.semaphore_signal(sem, inc=1, device_id=peer(step), device_id_type=MESH)
         pl.semaphore_signal(sem, inc=1, device_id=peer(-step), device_id_type=MESH)
 
-    signal_pair(barrier, z_peer, 1)
-    signal_pair(barrier, y_peer, 1)
+    for step in (2, 1):
+        signal_pair(barrier, z_peer, step)
+        signal_pair(barrier, y_peer, step)
 
     for load in loads:
         load.wait()
@@ -102,7 +103,7 @@
     padded_w = jnp.concatenate([weights, jnp.zeros((1, D - B_DEV), jnp.float32)], axis=1)
     q_all[g, B_DEV:Q_ROWS, :] = jnp.broadcast_to(padded_w, (Q_ROWS - B_DEV, D)).astype(jnp.bfloat16)
 
-    pl.semaphore_wait(barrier, 4 + 2 + 2)
+    pl.semaphore_wait(barrier, 4 + 4 + 4)
 
     def block_copy(buf, block, target, send_sem, recv_sem, index):
         return pltpu.make_async_remote_copy(
@@ -134,8 +135,8 @@
 
     first_sends(q_all, q_sems)
 
-    signal_pair(z_sems.at[0], z_peer, 1)
-    signal_pair(y_sems.at[0], y_peer, 1)
+    signal_pair(z_sems.at[0], z_peer, 2)
+    signal_pair(y_sem, y_peer, 2)
 
     owner_i = own_ref[...]
     row_i = row_ref[...]
@@ -186,8 +187,6 @@
     send(q_all, ahead_g, sib, q_sems, 5)
     pl.semaphore_wait(z_sems.at[0], 2)
     signal_pair(z_sems.at[1], z_peer, 2)
-    pl.semaphore_wait(y_sems.at[0], 2)
-    signal_pair(y_sems.at[1], y_peer, 2)
     block_logits(behind_g)
     block_logits(ahead_g)
     arrived(q_all, far_g, q_sems)
@@ -197,8 +196,6 @@
     arrived(q_all, other_core(ahead_x), q_sems)
     block_logits(other_core(ahead_x))
     block_logits(far_g)
-    pl.semaphore_wait(z_sems.at[1], 2)
-    signal_pair(z_sems.at[2], z_peer, 2)
     arrived(q_all, other_core(far_x), q_sems)
     block_logits(other_core(far_x))
 
@@ -225,8 +222,8 @@
         ids1_send[k] = ids1[k : k + 1]
     ids1_recv[z] = ids1_send[z]
 
-    pl.semaphore_wait(y_sems.at[1], 2)
-    pl.semaphore_wait(z_sems.at[2], 2)
+    pl.semaphore_wait(y_sem, 2)
+    pl.semaphore_wait(z_sems.at[1], 2)
 
     def ids1_copy(j):
         zt = jnp.where(z + j >= N_Z, z + j - N_Z, z + j)
@@ -460,7 +457,7 @@
             pltpu.VMEM((N_Z, 2 * N_Y, D), bf16),
             pltpu.VMEM((N_Y, 32, D), bf16),
             pltpu.VMEM((N_Y, 32, D), bf16),
-            dma((6,)), pltpu.SemaphoreType.REGULAR((3,)), pltpu.SemaphoreType.REGULAR((2,)),
+            dma((6,)), pltpu.SemaphoreType.REGULAR((2,)), pltpu.SemaphoreType.REGULAR,
             dma((7,)), dma((N_GRP,)),
             dma((N_GRP,)), dma((N_GRP,)),
             dma((N_X,)), dma((N_X,)), dma((N_X,)), dma((N_X,)),

time: 41.9 us -> 42 us (level)
  no operation moved by 1% of the time
where the time goes in v7:
time: 42 us; the launch traced here: 41.9 us
  Pallas kernels  41.2 us (98%)
  between operations  0.64 us (2%)
    pallas_call x1, Pallas kernels, shards(): pl.pallas_call(kernel, out_shape=(jax.ShapeDtypeStruct((B_DEV, D), bf16),...  40 us
    pallas_call x1, Pallas kernels, shards(): pl.pallas_call(write_out, out_shape=(jax.ShapeDtypeStruct((B_DEV, D), bf1...  1.24 us

profile of v7, /device:TPU:1, one launch (start us, length us, event | category | flops | bytes accessed | tf_op | source)
XLA Modules:
  0.0 41.9 jit_solution(10881630932022009852)
XLA Ops:
  0.6 40.0 %shard_map.77 = (bf16[128,256]{1,0:T(8,128)(2,1)S(1)}, bf16[256,256]{1,0:T(8,128)(2,1)S(1)}, bf16[1024,256]{1,0:T(8,128)(2,1)S(1)}, f32[1,256]{1,0:T(1,128)S(1)}) custom-call(bf16[128,256]{1,0:T(8,128)(2,1)} %q_hbm.1, bf16[160,256]{1,0:T(8,128)(2,1)} %it_hbm.1, bf16[160]{0:T(256)(128)(2,1)} %lq_hbm.1, bf16[128]{0:T(256)(128)(2,1)} %w_hbm.1, ...), custom_call_target="tpu_custom_call" | custom-call | tf_op jit(solution)/shard_map/pallas_call | solution.py:423
  40.6 1.2 %shard_map.78 = (bf16[128,256]{1,0:T(8,128)(2,1)}, f32[1024,256]{1,0:T(8,128)}) custom-call(bf16[128,256]{1,0:T(8,128)(2,1)S(1)} %get-tuple-element.6.query_ref, bf16[256,256]{1,0:T(8,128)(2,1)S(1)} %get-tuple-element.7.rows_ref, bf16[1024,256]{1,0:T(8,128)(2,1)S(1)} %get-tuple-element.8.member_ref, f32[1,256]{1,0:T(1,128)S(1)} %get-tuple-element.9.norm_ref), custom_call_target="tpu_custom_call" | custom-call | tf_op jit(solution)/shard_map/pallas_call | solution.py:481
